TPU v7x, 32 devices: a whole 2x2x4 slice. The times are simulated.
32 devices in a mesh: dp: 8 (over y, x, core), shard: 4 (over z).
Axes of the slice: x: 2, y: 2, z: 4, core: 2. Of those that a mesh axis runs over, the one named last changes fastest.
Arguments:
- tokens: bfloat16 [32768, 768], P(('dp', 'shard'))
- out_grad: bfloat16 [32768, 768], P(('dp', 'shard'))
- first_lengths: int32 [32], P(('dp', 'shard')), may hold values from 512 to 1024, as said below
- quant_scales: float32 [6], replicated, as said below
- attn_quant: bfloat16 [768, 3072], P('dp', 'shard'), may hold values from -127 to 127
- up_quant: bfloat16 [768, 3072], P('dp', 'shard'), may hold values from -127 to 127
- down_quant: bfloat16 [3072, 768], P('dp', 'shard'), may hold values from -127 to 127
- attn_master: float32 [768, 3072], P('dp', 'shard'), as said below
- attn_first: float32 [768, 3072], P('dp', 'shard')
- attn_second: float32 [768, 3072], P('dp', 'shard'), as said below
- attn_average: float32 [768, 3072], P('dp', 'shard'), may hold values from -0.21875 to 0.21875
- up_master: float32 [768, 3072], P('dp', 'shard'), as said below
- up_first: float32 [768, 3072], P('dp', 'shard')
- up_second: float32 [768, 3072], P('dp', 'shard'), as said below
- up_average: float32 [768, 3072], P('dp', 'shard'), may hold values from -0.21875 to 0.21875
- down_master: float32 [3072, 768], P('dp', 'shard'), as said below
- down_first: float32 [3072, 768], P('dp', 'shard')
- down_second: float32 [3072, 768], P('dp', 'shard'), as said below
- down_average: float32 [3072, 768], P('dp', 'shard'), may hold values from -0.109375 to 0.109375
- vector_master: float32 [768, 12], P('dp', 'shard')
- vector_first: float32 [768, 12], P('dp', 'shard')
- vector_second: float32 [768, 12], P('dp', 'shard'), as said below
- vector_average: float32 [768, 12], P('dp', 'shard'), may hold values from -3 to 3
Outputs:
- layer_out: bfloat16 [32768, 768], P(('dp', 'shard'))
- input_grad: bfloat16 [32768, 768], P(('dp', 'shard'))
- grad_norm: float32 [], replicated
- attn_first_new: float32 [768, 3072], P('dp', 'shard')
- attn_second_new: float32 [768, 3072], P('dp', 'shard')
- attn_master_new: float32 [768, 3072], P('dp', 'shard')
- attn_average_new: float32 [768, 3072], P('dp', 'shard')
- up_first_new: float32 [768, 3072], P('dp', 'shard')
- up_second_new: float32 [768, 3072], P('dp', 'shard')
- up_master_new: float32 [768, 3072], P('dp', 'shard')
- up_average_new: float32 [768, 3072], P('dp', 'shard')
- down_first_new: float32 [3072, 768], P('dp', 'shard')
- down_second_new: float32 [3072, 768], P('dp', 'shard')
- down_master_new: float32 [3072, 768], P('dp', 'shard')
- down_average_new: float32 [3072, 768], P('dp', 'shard')
- vector_first_new: float32 [768, 12], P('dp', 'shard')
- vector_second_new: float32 [768, 12], P('dp', 'shard')
- vector_master_new: float32 [768, 12], P('dp', 'shard')
- vector_average_new: float32 [768, 12], P('dp', 'shard')
Inputs may be any that keep to these rules, and one draw needn't show every extreme that they name: `first_lengths`: each buffer of 1024 rows holds one sequence of 1024 tokens (value 1024) or two of 512 tokens (value 1024 / 2); both kinds occur in every draw. `quant_scales`: positive. `attn_master`: each entry within half a quantization step of the integer copy times its scale. `up_master`: each entry within half a quantization step of the integer copy times its scale. `down_master`: each entry within half a quantization step of the integer copy times its scale. `attn_second`: positive. `up_second`: positive. `down_second`: positive. `vector_second`: positive.
All inputs are finite; a program needn't handle non-finite values.
Results may differ from a plain program's by a relative error of at most 0.012.
Values may be sent and summed in bfloat16 or wider, within the bound.
No kernel may reach another device: no remote copies, remote signals or barrier semaphores. Data moves between devices by JAX's collectives and lax.ppermute only.
A program may use at most 256 MiB of HBM per device.

v0:
```python
import math

import jax
import jax.numpy as jnp
from jax import lax
from jax.sharding import PartitionSpec as P

HEADS = 12
HEAD_DIM = 64
STEP = 10


norm_eps = 1e-06
clip_limit = 1.0
beta_first = 0.9
beta_second = 0.999
adam_eps = 1e-08
matrix_rate = 0.08
vector_rate = 0.5
matrix_decay = 0.01
average_keep = 0.9


def contract_last(left, right):
    return lax.dot_general(
        left, right, (((1,), (1,)), ((), ())), preferred_element_type=jnp.float32
    )


def contract_first(left, right):
    return lax.dot_general(
        left, right, (((0,), (0,)), ((), ())), preferred_element_type=jnp.float32
    )


def norm_forward(inputs, gain_row, shift_row):
    centre = inputs - jnp.mean(inputs, axis=-1, keepdims=True)
    inv_std = lax.rsqrt(jnp.mean(centre * centre, axis=-1, keepdims=True) + norm_eps)
    normed = centre * inv_std
    return (normed * gain_row + shift_row, normed, inv_std)


def norm_backward(grad_out, normed, inv_std, gain_row):
    scaled = grad_out * gain_row
    return inv_std * (
        scaled
        - jnp.mean(scaled, axis=-1, keepdims=True)
        - normed * jnp.mean(scaled * normed, axis=-1, keepdims=True)
    )


def adam_update(gradient, master, first_old, second_old, average, step_rate, decay_rate):
    first_new = beta_first * first_old + (1.0 - beta_first) * gradient
    second_new = beta_second * second_old + (1.0 - beta_second) * gradient * gradient
    first_hat = first_new / (1.0 - beta_first**STEP)
    second_hat = second_new / (1.0 - beta_second**STEP)
    master_new = master - step_rate * (
        first_hat / (jnp.sqrt(second_hat) + adam_eps) + decay_rate * master
    )
    average_new = average_keep * average + (1.0 - average_keep) * master_new
    return (first_new, second_new, master_new, average_new)


def on_device(
    tokens,
    out_grad,
    first_lengths,
    quant_scales,
    attn_quant,
    up_quant,
    down_quant,
    attn_master,
    attn_first,
    attn_second,
    attn_average,
    up_master,
    up_first,
    up_second,
    up_average,
    down_master,
    down_first,
    down_second,
    down_average,
    vector_master,
    vector_first,
    vector_second,
    vector_average,
):
    model_width = tokens.shape[1]
    tok_count = tokens.shape[0]
    vector_low = vector_master.astype(jnp.bfloat16)
    attn_part, up_part, down_part, vector_part = (
        lax.all_gather(attn_quant, "shard", axis=1, tiled=True),
        lax.all_gather(up_quant, "shard", axis=1, tiled=True),
        lax.all_gather(down_quant, "shard", axis=1, tiled=True),
        lax.all_gather(vector_low, "shard", axis=1, tiled=True),
    )
    attn_w, up_w, down_w, vector_w = (
        lax.all_gather(attn_part, "dp", axis=0, tiled=True),
        lax.all_gather(up_part, "dp", axis=0, tiled=True),
        lax.all_gather(down_part, "dp", axis=0, tiled=True),
        lax.all_gather(vector_part, "dp", axis=0, tiled=True),
    )
    vectors = vector_w.astype(jnp.float32)
    bias_q = vectors[:, 0]
    bias_v = vectors[:, 1]
    bias_o = vectors[:, 2]
    gain_one = vectors[:, 3]
    shift_one = vectors[:, 4]
    bias_two = vectors[:, 5]
    gain_two = vectors[:, 6]
    shift_two = vectors[:, 7]
    bias_up = vectors[:, 8:].T.reshape(-1)
    inputs = tokens.astype(jnp.float32)
    column_scale = jnp.repeat(quant_scales[:3], model_width)
    qkv_raw = (
        jnp.dot(tokens, attn_w[:, : 3 * model_width], preferred_element_type=jnp.float32)
        * column_scale
    )
    queries = (qkv_raw[:, :model_width] + bias_q).astype(jnp.bfloat16)
    key_rows = qkv_raw[:, model_width : 2 * model_width].astype(jnp.bfloat16)
    values = (qkv_raw[:, 2 * model_width :] + bias_v).astype(jnp.bfloat16)
    q_heads = queries.reshape(tok_count, HEADS, HEAD_DIM)
    k_heads = key_rows.reshape(tok_count, HEADS, HEAD_DIM)
    v_heads = values.reshape(tok_count, HEADS, HEAD_DIM)
    position = jnp.arange(tok_count, dtype=jnp.int32)
    segment = (position >= first_lengths[0]).astype(jnp.int32)
    block_rows = min(512, tok_count)
    block_total = tok_count // block_rows
    inv_root = 1.0 / math.sqrt(HEAD_DIM)

    def block_scores(start):
        q_part = q_heads[start : start + block_rows]
        raw_scores = jnp.einsum("qhd,khd->hqk", q_part, k_heads, preferred_element_type=jnp.float32)
        same_seq = segment[start : start + block_rows, None] == segment[None, :]
        return (jnp.where(same_seq[None], raw_scores * inv_root, -1e30), q_part)

    context_parts = []
    log_sums = []
    for block_index in range(block_total):
        scores, q_part = block_scores(block_index * block_rows)
        row_max = jnp.max(scores, axis=-1, keepdims=True)
        exponent = jnp.exp(scores - row_max)
        row_total = jnp.sum(exponent, axis=-1, keepdims=True)
        attn_prob = exponent / row_total
        log_sums.append(row_max + jnp.log(row_total))
        context_parts.append(
            jnp.einsum(
                "hqk,khd->qhd",
                attn_prob.astype(jnp.bfloat16),
                v_heads,
                preferred_element_type=jnp.float32,
            )
        )
    context = (
        jnp.concatenate(context_parts, axis=0).reshape(tok_count, model_width).astype(jnp.bfloat16)
    )
    out_proj = attn_w[:, 3 * model_width :]
    residual_one = (
        inputs
        + jnp.dot(context, out_proj, preferred_element_type=jnp.float32) * quant_scales[3]
        + bias_o
    )
    norm_one, normed_one, inv_one = norm_forward(residual_one, gain_one, shift_one)
    norm_one_low = norm_one.astype(jnp.bfloat16)
    hidden = (
        jnp.dot(norm_one_low, up_w, preferred_element_type=jnp.float32) * quant_scales[4] + bias_up
    )
    gelu_out, gelu_back = jax.vjp(lambda inner: jax.nn.gelu(inner, approximate=True), hidden)
    activated = gelu_out.astype(jnp.bfloat16)
    residual_two = (
        norm_one
        + jnp.dot(activated, down_w, preferred_element_type=jnp.float32) * quant_scales[5]
        + bias_two
    )
    layer_float, normed_two, inv_two = norm_forward(residual_two, gain_two, shift_two)
    layer_out = layer_float.astype(jnp.bfloat16)
    grad_output = out_grad.astype(jnp.float32)
    grad_gain_two = jnp.sum(grad_output * normed_two, axis=0)
    grad_shift_two = jnp.sum(grad_output, axis=0)
    d_total = norm_backward(grad_output, normed_two, inv_two, gain_two)
    grad_bias_two = jnp.sum(d_total, axis=0)
    d_total_low = d_total.astype(jnp.bfloat16)
    grad_down = contract_first(activated, d_total_low)
    d_active = contract_last(d_total_low, down_w) * quant_scales[5]
    d_hidden = gelu_back(d_active)[0]
    grad_bias_up = jnp.sum(d_hidden, axis=0)
    d_hidden_low = d_hidden.astype(jnp.bfloat16)
    grad_up = contract_first(norm_one_low, d_hidden_low)
    d_norm_one = d_total + contract_last(d_hidden_low, up_w) * quant_scales[4]
    grad_gain_one = jnp.sum(d_norm_one * normed_one, axis=0)
    grad_shift_one = jnp.sum(d_norm_one, axis=0)
    d_residual = norm_backward(d_norm_one, normed_one, inv_one, gain_one)
    grad_bias_o = jnp.sum(d_residual, axis=0)
    d_residual_low = d_residual.astype(jnp.bfloat16)
    grad_out_proj = contract_first(context, d_residual_low)
    d_context = (contract_last(d_residual_low, out_proj) * quant_scales[3]).astype(jnp.bfloat16)
    d_ctx_heads = d_context.reshape(tok_count, HEADS, HEAD_DIM)
    grad_values = jnp.zeros((tok_count, HEADS, HEAD_DIM), jnp.float32)
    grad_keys = jnp.zeros((tok_count, HEADS, HEAD_DIM), jnp.float32)
    query_grads = []
    for block_index in range(block_total):
        start = block_index * block_rows
        scores, q_part = block_scores(start)
        attn_prob = jnp.exp(scores - log_sums[block_index])
        d_part = d_ctx_heads[start : start + block_rows]
        grad_values = grad_values + jnp.einsum(
            "hqk,qhd->khd",
            attn_prob.astype(jnp.bfloat16),
            d_part,
            preferred_element_type=jnp.float32,
        )
        d_prob = jnp.einsum("qhd,khd->hqk", d_part, v_heads, preferred_element_type=jnp.float32)
        row_dot = jnp.sum(attn_prob * d_prob, axis=-1, keepdims=True)
        d_scores = (attn_prob * (d_prob - row_dot) * inv_root).astype(jnp.bfloat16)
        query_grads.append(
            jnp.einsum("hqk,khd->qhd", d_scores, k_heads, preferred_element_type=jnp.float32)
        )
        grad_keys = grad_keys + jnp.einsum(
            "hqk,qhd->khd", d_scores, q_part, preferred_element_type=jnp.float32
        )
    grad_query = jnp.concatenate(query_grads, axis=0).reshape(tok_count, model_width)
    grad_key = grad_keys.reshape(tok_count, model_width)
    grad_value = grad_values.reshape(tok_count, model_width)
    d_qkv = jnp.concatenate([grad_query, grad_key, grad_value], axis=1).astype(jnp.bfloat16)
    grad_qkv = contract_first(tokens, d_qkv)
    grad_attn = jnp.concatenate([grad_qkv, grad_out_proj], axis=1)
    d_inputs = d_residual
    for part_index in range(3):
        lower_edge = part_index * model_width
        upper_edge = lower_edge + model_width
        d_inputs = (
            d_inputs
            + contract_last(d_qkv[:, lower_edge:upper_edge], attn_w[:, lower_edge:upper_edge])
            * quant_scales[part_index]
        )
    input_grad = d_inputs.astype(jnp.bfloat16)
    vector_cols = jnp.stack(
        [
            jnp.sum(grad_query, axis=0),
            jnp.sum(grad_value, axis=0),
            grad_bias_o,
            grad_gain_one,
            grad_shift_one,
            grad_bias_two,
            grad_gain_two,
            grad_shift_two,
        ],
        axis=1,
    )
    grad_vector = jnp.concatenate([vector_cols, grad_bias_up.reshape(-1, model_width).T], axis=1)
    row_attn, row_up, row_down, row_vector = (
        lax.psum_scatter(grad_attn, "dp", scatter_dimension=0, tiled=True),
        lax.psum_scatter(grad_up, "dp", scatter_dimension=0, tiled=True),
        lax.psum_scatter(grad_down, "dp", scatter_dimension=0, tiled=True),
        lax.psum_scatter(grad_vector, "dp", scatter_dimension=0, tiled=True),
    )
    own_attn, own_up, own_down, own_vector = (
        lax.psum_scatter(
            row_attn.astype(jnp.bfloat16), "shard", scatter_dimension=1, tiled=True
        ).astype(jnp.float32),
        lax.psum_scatter(
            row_up.astype(jnp.bfloat16), "shard", scatter_dimension=1, tiled=True
        ).astype(jnp.float32),
        lax.psum_scatter(
            row_down.astype(jnp.bfloat16), "shard", scatter_dimension=1, tiled=True
        ).astype(jnp.float32),
        lax.psum_scatter(
            row_vector.astype(jnp.bfloat16), "shard", scatter_dimension=1, tiled=True
        ).astype(jnp.float32),
    )
    local_squares = (
        jnp.sum(own_attn * own_attn)
        + jnp.sum(own_up * own_up)
        + jnp.sum(own_down * own_down)
        + jnp.sum(own_vector * own_vector)
    )
    grad_norm = jnp.sqrt(lax.psum(local_squares, ("dp", "shard")))
    factor = jnp.minimum(1.0, clip_limit / (grad_norm + norm_eps))
    attn_a, attn_b, attn_c, attn_d = adam_update(
        own_attn * factor,
        attn_master,
        attn_first,
        attn_second,
        attn_average,
        matrix_rate,
        matrix_decay,
    )
    up_a, up_b, up_c, up_d = adam_update(
        own_up * factor, up_master, up_first, up_second, up_average, matrix_rate, matrix_decay
    )
    down_a, down_b, down_c, down_d = adam_update(
        own_down * factor,
        down_master,
        down_first,
        down_second,
        down_average,
        matrix_rate,
        matrix_decay,
    )
    vector_a, vector_b, vector_c, vector_d = adam_update(
        own_vector * factor,
        vector_master,
        vector_first,
        vector_second,
        vector_average,
        vector_rate,
        0.0,
    )
    return (
        layer_out,
        input_grad,
        grad_norm,
        attn_a,
        attn_b,
        attn_c,
        attn_d,
        up_a,
        up_b,
        up_c,
        up_d,
        down_a,
        down_b,
        down_c,
        down_d,
        vector_a,
        vector_b,
        vector_c,
        vector_d,
    )


def solution(mesh):
    in_specs = (
        P(("dp", "shard"), None),
        P(("dp", "shard"), None),
        P(("dp", "shard")),
        P(),
        P("dp", "shard"),
        P("dp", "shard"),
        P("dp", "shard"),
        P("dp", "shard"),
        P("dp", "shard"),
        P("dp", "shard"),
        P("dp", "shard"),
        P("dp", "shard"),
        P("dp", "shard"),
        P("dp", "shard"),
        P("dp", "shard"),
        P("dp", "shard"),
        P("dp", "shard"),
        P("dp", "shard"),
        P("dp", "shard"),
        P("dp", "shard"),
        P("dp", "shard"),
        P("dp", "shard"),
        P("dp", "shard"),
    )
    out_specs = (
        P(("dp", "shard"), None),
        P(("dp", "shard"), None),
        P(),
        P("dp", "shard"),
        P("dp", "shard"),
        P("dp", "shard"),
        P("dp", "shard"),
        P("dp", "shard"),
        P("dp", "shard"),
        P("dp", "shard"),
        P("dp", "shard"),
        P("dp", "shard"),
        P("dp", "shard"),
        P("dp", "shard"),
        P("dp", "shard"),
        P("dp", "shard"),
        P("dp", "shard"),
        P("dp", "shard"),
        P("dp", "shard"),
    )
    return jax.shard_map(
        on_device, mesh=mesh, in_specs=in_specs, out_specs=out_specs, check_vma=False
    )
```

profile of v0, /device:TPU:0, one launch (start us, length us, event | category | flops | bytes accessed | tf_op | source)
XLA Modules:
  0.0 871.9 jit_solution(11041361839649555202)
XLA Ops:
  7.3 20.4 %all_gather.24 = bf16[96,3072]{1,0:T(8,128)(2,1)} all-gather(bf16[96,768]{1,0:T(8,128)(2,1)} %param.27), channel_id=1, replica_groups=mesh['dp'=8,'shard'=4] {'shard'}, dimensions={1}, use_global_device_ids=true | all-gather | bytes 737280 | tf_op jit(solution)/shard_map/all_gather | solution.py:93
  27.8 17.0 %all_gather.28 = bf16[96,3072]{1,0:T(8,128)(2,1)} all-gather(bf16[96,768]{1,0:T(8,128)(2,1)} %param.28), channel_id=1, replica_groups=mesh['dp'=8,'shard'=4] {'shard'}, dimensions={1}, use_global_device_ids=true | all-gather | bytes 737280 | tf_op jit(solution)/shard_map/all_gather | solution.py:94
  44.8 17.3 %all_gather.30 = bf16[384,768]{0,1:T(8,128)(2,1)} all-gather(bf16[384,192]{0,1:T(8,128)(2,1)} %param.29), channel_id=1, replica_groups=mesh['dp'=8,'shard'=4] {'shard'}, dimensions={1}, use_global_device_ids=true | all-gather | bytes 737280 | tf_op jit(solution)/shard_map/all_gather | solution.py:95
  62.9 9.8 %all-gather = bf16[4,3,96]{2,1,0:T(4,128)(2,1)S(1)} all-gather(bf16[1,3,96]{2,1,0:T(4,128)(2,1)S(1)} %convert_bitcast_fusion), channel_id=1, replica_groups=mesh['dp'=8,'shard'=4] {'shard'}, dimensions={0}, use_global_device_ids=true | all-gather | bytes 2880 | tf_op jit(solution)/shard_map/all_gather | solution.py:96
  72.7 9.2 %all-gather.1 = bf16[8,96,12]{1,2,0:T(8,128)(2,1)S(1)} all-gather(bf16[1,96,12]{1,2,0:T(8,128)(2,1)S(1)} %bitcast.115), channel_id=1, replica_groups=mesh['dp'=8,'shard'=4] {'dp'}, dimensions={0}, use_global_device_ids=true | all-gather | bytes 20736 | tf_op jit(solution)/shard_map/all_gather | solution.py:102
  86.1 1.6 copy.182
  87.8 1.6 copy.175
  89.4 1.6 broadcast_compare_fusion.1
  91.0 5.9 convolution_multiply_fusion
  96.9 3.6 copy-done.11
  101.5 5.1 fusion.49
  109.2 1.7 copy.177
  110.9 12.3 %fusion.7 = (f32[12,512]{1,0:T(8,128)S(1)}, f32[12,512,1024]{2,1,0:T(8,128)}) fusion(pred[512,1024]{1,0:T(8,128)(4,1)} %get-tuple-element.138, bf16[512,12,64]{0,2,1:T(8,128)(2,1)} %bitcast.104, bf16[1024,12,64]{0,2,1:T(8,128)(2,1)S(1)} %bitcast.94), kind=kOutput, calls=%fused_computation.21 | convolution fusion | flops 824174592 | bytes 28073984 | tf_op jit(solution)/shard_map/qhd,khd->hqk/dot_general | solution.py:134
  123.2 11.1 %fusion.6 = (f32[12,512]{1,0:T(8,128)S(1)}, f32[12,512,1024]{2,1,0:T(8,128)}) fusion(pred[512,1024]{1,0:T(8,128)(4,1)S(1)} %copy-done.16, bf16[512,12,64]{0,2,1:T(8,128)(2,1)S(1)} %bitcast.102, bf16[1024,12,64]{0,2,1:T(8,128)(2,1)S(1)} %bitcast.95), kind=kOutput, calls=%fused_computation.20 | convolution fusion | flops 824174592 | bytes 28073984 | tf_op jit(solution)/shard_map/qhd,khd->hqk/dot_general | solution.py:134
  134.3 21.2 %fusion.4 = (f32[12,512]{1,0:T(8,128)S(1)}, f32[12,512]{1,0:T(8,128)S(1)}) fusion(f32[12,512,1024]{2,1,0:T(8,128)} %get-tuple-element.150, f32[12,512]{1,0:T(8,128)S(1)} %get-tuple-element.149, pred[512,1024]{1,0:T(8,128)(4,1)S(1)} %copy-done.16, f32[12,512]{1,0:T(8,128)S(1)} %get-tuple-element.147, f32[12,512,1024]{2,1,0:T(8,128)} %get-tuple-element.148, ...), kind=kLoop, calls=%fused_computation.16 | loop fusion | flops 50319360 | bytes 51478528 | tf_op jit(solution)/shard_map/reduce_sum | solution.py:144
  155.5 13.8 %fusion.66 = bf16[512,12,64]{0,2,1:T(8,128)(2,1)} fusion(bf16[1024,12,64]{0,2,1:T(8,128)(2,1)S(1)} %bitcast.90, f32[12,512,1024]{2,1,0:T(8,128)} %get-tuple-element.148, f32[12,512]{1,0:T(8,128)S(1)} %get-tuple-element.165, f32[12,512]{1,0:T(8,128)S(1)} %get-tuple-element.147, pred[512,1024]{1,0:T(8,128)(4,1)S(1)} %copy-done.18), kind=kOutput, calls=%fused_computation.97 | convolution fusion | flops 837156864 | bytes 28098560 | tf_op jit(solution)/shard_map/hqk,khd->qhd/dot_general | solution.py:148
  169.3 8.5 fusion.65
  179.2 3.8 fusion.145
  183.1 1.6 copy-done
  185.1 11.0 %fusion.127 = f32[1024,3072]{1,0:T(8,128)} fusion(bf16[768,3072]{1,0:T(8,128)(2,1)} %all-gather.8.cloned.1.call-done, f32[1024,768]{0,1:T(8,128)} %copy-done, f32[768]{0:T(1024)S(1)} %copy-done.39, f32[768]{0:T(1024)S(1)} %copy-done.38, f32[1024]{0:T(1024)S(1)} %add_rsqrt_fusion.1, f32[1024]{0:T(1024)S(1)} %broadcast_multiply_fusion.5), kind=kOutput, calls=%fused_computation.194 | convolution fusion | flops 4835770368 | bytes 20461568 | tf_op jit(solution)/shard_map/dot_general | solution.py:167
  196.2 12.7 %fusion.146 = (f32[1024]{0:T(1024)S(1)}, f32[1024,768]{0,1:T(8,128)S(1)}) fusion(f32[768]{0:T(1024)S(1)} %copy-done.56, f32[]{:T(128)} %bitcast.15, bf16[3072,768]{0,1:T(8,128)(2,1)} %all-gather.10.cloned.1.call-done, f32[1024,3072]{1,0:T(8,128)} %fusion.127, f32[3072]{0:T(1024)S(1)} %copy-done.52, f32[]{:T(128)} %bitcast.13, f32[768]{0:T(1024)S(1)} %copy-done.39, ...), kind=kOutput, calls=%fused_computation.202 | convolution fusion | flops 4872731648 | bytes 23626760 | tf_op jit(solution)/shard_map/dot_general | solution.py:173
  210.3 20.9 %fusion.151 = (f32[3072]{0:T(1024)}, bf16[1024,3072]{1,0:T(8,128)(2,1)}) fusion(f32[3072]{0:T(1024)S(1)} %copy-done.52, f32[1024,3072]{1,0:T(8,128)} %fusion.127, f32[]{:T(128)} %bitcast.13, f32[]{:T(128)} %bitcast.15, bf16[3072,768]{0,1:T(8,128)(2,1)S(1)} %bitcast.117, f32[1024]{0:T(1024)S(1)} %broadcast_multiply_fusion.2, ...), kind=kOutput, calls=%fused_computation.203 | convolution fusion | flops 4914410496 | bytes 28355592 | tf_op jit(solution)/shard_map/dot_general | solution.py:25
  231.2 10.5 %fusion.51 = f32[768,3072]{1,0:T(8,128)} fusion(bf16[1024,3072]{1,0:T(8,128)(2,1)} %get-tuple-element.163, f32[1024,768]{0,1:T(8,128)S(1)} %copy-done.1, f32[768]{0:T(1024)S(1)} %copy-done.39, f32[768]{0:T(1024)S(1)} %copy-done.38, f32[1024]{0:T(1024)S(1)} %add_rsqrt_fusion.1, f32[1024]{0:T(1024)S(1)} %broadcast_multiply_fusion.5), kind=kOutput, calls=%fused_computation.73 | convolution fusion | flops 4835770368 | bytes 18888704
  241.8 14.4 %multiply_reduce_fusion.2 = (f32[768]{0:T(1024)}, f32[1024]{0:T(1024)S(1)}, f32[1024]{0:T(1024)S(1)}, f32[768]{0:T(1024)}, f32[1024,768]{0,1:T(8,128)S(1)}) fusion(f32[1024,768]{0,1:T(8,128)} %copy-done, f32[1024]{0:T(1024)S(1)} %add_rsqrt_fusion.1, f32[1024]{0:T(1024)S(1)} %broadcast_multiply_fusion.5, f32[768]{0:T(1024)S(1)} %copy-done.38, f32[]{:T(128)} %bitcast.13, ...), kind=kOutput, calls=%fused_computation.66 | convolution fusion | flops 4846776320 | bytes 22065156 | tf_op jit(solution)/shard_map/dot_general | solution.py:25
  256.2 1.7 fusion.140
  258.0 3.8 multiply_convert_fusion.3
  263.6 10.5 %fusion.152 = f32[12,512,1024]{2,1,0:T(8,128)} fusion(bf16[512,12,64]{0,2,1:T(8,128)(2,1)S(1)} %bitcast.98, bf16[1024,12,64]{0,2,1:T(8,128)(2,1)S(1)} %bitcast.92), kind=kOutput, calls=%fused_computation.204 | convolution fusion | flops 805306368 | bytes 27525120 | tf_op jit(solution)/shard_map/qhd,khd->hqk/dot_general | solution.py:213
  274.2 52.5 %bitcast_convert_fusion.2 = (bf16[512,12,64]{0,2,1:T(8,128)(2,1)}, f32[12,64,512]{2,1,0:T(8,128)}) fusion(bf16[1024,12,64]{0,2,1:T(8,128)(2,1)S(1)} %bitcast.96, f32[12,512,1024]{2,1,0:T(8,128)} %fusion.152, f32[12,512]{1,0:T(8,128)S(1)} %log_add_fusion.1, f32[12,512,1024]{2,1,0:T(8,128)} %get-tuple-element.150, pred[512,1024]{1,0:T(8,128)(4,1)} %get-tuple-element.137), kind=kOutput, calls=%fused_computation.93 | convolution fusion | flops 874912768 | bytes 54812672 | tf_op jit(solution)/shard_map/hqk,khd->qhd/dot_general | solution.py:217
  326.7 11.7 %fusion.153 = f32[12,512,1024]{2,1,0:T(8,128)} fusion(bf16[512,12,64]{0,2,1:T(8,128)(2,1)} %bitcast.100, bf16[1024,12,64]{0,2,1:T(8,128)(2,1)S(1)} %bitcast.93), kind=kOutput, calls=%fused_computation.205 | convolution fusion | flops 805306368 | bytes 27525120 | tf_op jit(solution)/shard_map/qhd,khd->hqk/dot_general | solution.py:213
  338.3 51.9 %bitcast_convert_fusion.1 = (bf16[512,12,64]{0,2,1:T(8,128)(2,1)}, f32[12,64,512]{2,1,0:T(8,128)}) fusion(bf16[1024,12,64]{0,2,1:T(8,128)(2,1)S(1)} %bitcast.97, f32[12,512,1024]{2,1,0:T(8,128)} %fusion.153, f32[12,512]{1,0:T(8,128)S(1)} %log_add_fusion, f32[12,512,1024]{2,1,0:T(8,128)} %get-tuple-element.148, pred[512,1024]{1,0:T(8,128)(4,1)} %get-tuple-element.138), kind=kOutput, calls=%fused_computation.91 | convolution fusion | flops 874912768 | bytes 54812672 | tf_op jit(solution)/shard_map/hqk,khd->qhd/dot_general | solution.py:217
  390.2 2.4 pad_maximum_fusion.2
  392.7 53.4 %fusion.25 = f32[12,64,1024]{2,1,0:T(8,128)} fusion(bf16[512,12,64]{0,2,1:T(8,128)(2,1)S(1)} %bitcast.103, f32[12,512,1024]{2,1,0:T(8,128)} %fusion.152, f32[12,512]{1,0:T(8,128)S(1)} %log_add_fusion.1, f32[12,512,1024]{2,1,0:T(8,128)} %get-tuple-element.150, pred[512,1024]{1,0:T(8,128)(4,1)} %get-tuple-element.137), kind=kOutput, calls=%fused_computation.36 | convolution fusion | flops 874519552 | bytes 54812672 | tf_op jit(solution)/shard_map/hqk,qhd->khd/dot_general | solution.py:219
  446.1 48.3 %add_convert_fusion.1 = bf16[12,64,1024]{2,1,0:T(8,128)(2,1)} fusion(f32[12,64,1024]{2,1,0:T(8,128)} %fusion.25, bf16[512,12,64]{0,2,1:T(8,128)(2,1)} %bitcast.105, f32[12,512,1024]{2,1,0:T(8,128)} %fusion.153, f32[12,512]{1,0:T(8,128)S(1)} %log_add_fusion, f32[12,512,1024]{2,1,0:T(8,128)} %get-tuple-element.148, pred[512,1024]{1,0:T(8,128)(4,1)} %get-tuple-element.138), kind=kOutput, calls=%fused_computation.68 | convolution fusion | flops 876092416 | bytes 56385536 | tf_op jit(solution)/shard_map/hqk,qhd->khd/dot_general | solution.py:219
  494.4 4.3 fusion.74
  498.7 11.5 %fusion.14 = f32[12,64,1024]{2,1,0:T(8,128)S(1)} fusion(bf16[512,12,64]{0,2,1:T(8,128)(2,1)S(1)} %bitcast.101, f32[12,512,1024]{2,1,0:T(8,128)} %get-tuple-element.148, f32[12,512]{1,0:T(8,128)S(1)} %log_add_fusion, pred[512,1024]{1,0:T(8,128)(4,1)S(1)} %copy-done.19), kind=kOutput, calls=%fused_computation.28 | convolution fusion | flops 830472192 | bytes 29646848 | tf_op jit(solution)/shard_map/hqk,qhd->khd/dot_general | solution.py:207
  510.3 13.7 %bitcast_convert_fusion = (bf16[1024,12,64]{0,2,1:T(8,128)(2,1)S(1)}, f32[12,64,1024]{2,1,0:T(8,128)}) fusion(f32[12,64,1024]{2,1,0:T(8,128)S(1)} %fusion.14, bf16[512,12,64]{0,2,1:T(8,128)(2,1)S(1)} %bitcast.99, f32[12,512]{1,0:T(8,128)S(1)} %log_add_fusion.1, f32[12,512,1024]{2,1,0:T(8,128)} %get-tuple-element.150, pred[512,1024]{1,0:T(8,128)(4,1)S(1)} %copy-done.17), kind=kOutput, calls=%fused_computation.65 | convolution fusion | flops 832045056 | bytes 34365440 | tf_op jit(solution)/shard_map/hqk,qhd->khd/dot_general | solution.py:207
  525.2 9.3 %convolution_bitcast_fusion = f32[768,2304]{0,1:T(8,128)} fusion(bf16[1024,768]{1,0:T(8,128)(2,1)S(1)} %copy-done.26, bf16[1024,768]{0,1:T(8,128)(2,1)S(1)} %bitcast.111, bf16[1024,768]{0,1:T(8,128)(2,1)S(1)} %bitcast.119, bf16[1024,768]{0,1:T(8,128)(2,1)S(1)} %bitcast.107), kind=kOutput, calls=%fused_computation.42 | convolution fusion | flops 3638034432 | bytes 13369344 | tf_op jit(solution)/shard_map/dot_general | solution.py:31
  534.5 7.2 pad_maximum_fusion
  541.7 9.6 %copy.199 = f32[768,3072]{1,0:T(8,128)} copy(f32[768,3072]{0,1:T(8,128)} %pad_maximum_fusion) | data formatting | bytes 18874368
  551.4 1.8 copy-done.4
  553.2 16.4 %fusion.77 = f32[3072,768]{1,0:T(8,128)} fusion(bf16[1024,768]{0,1:T(8,128)(2,1)} %copy.182, f32[1024,768]{0,1:T(8,128)S(1)} %copy-done.4, f32[1024]{0:T(1024)S(1)} %broadcast_multiply_fusion.2, f32[1024]{0:T(1024)S(1)} %broadcast_multiply_fusion.3, f32[768]{0:T(1024)S(1)} %copy-done.49, f32[1024]{0:T(1024)S(1)} %add_rsqrt_fusion, ...), kind=kOutput, calls=%fused_computation.110 | convolution fusion | flops 4873519104 | bytes 26770436 | tf_op jit(solution)/shard_map/dot_general | solution.py:31
  570.3 4.1 fusion.48
  574.5 2.7 bitcast_reduce_fusion
  577.3 1.7 bitcast_reduce_fusion.2
  580.4 2.2 convert_element_type.121
  582.7 43.9 %reduce-scatter.22.cloned.1.call-done = f32[96,3072]{1,0:T(8,128)} async-done(((f32[768,3072]{1,0:T(8,128)}), f32[96,3072]{1,0:T(8,128)}) %reduce-scatter.22.cloned.1.call-update) | async-done | bytes 1179664 | tf_op jit(solution)/shard_map/reduce_scatter | solution.py:253
  626.5 2.2 convert_element_type.119
  630.0 1.8 copy.191
  631.8 4.4 fusion.70
  636.2 70.2 %reduce-scatter.20.cloned.1.call-done = f32[384,768]{1,0:T(8,128)} async-done(((f32[3072,768]{1,0:T(8,128)}), f32[384,768]{1,0:T(8,128)}) %reduce-scatter.20.cloned.1.call-update) | async-done | bytes 1179664 | tf_op jit(solution)/shard_map/reduce_scatter | solution.py:255
  708.9 3.3 fusion.68
  713.0 4.8 add_convert_fusion
  717.8 25.6 %reduce-scatter.28.cloned.1.call-done = f32[96,12]{1,0:T(8,128)} async-done(((f32[768,12]{1,0:T(8,128)}), f32[96,12]{1,0:T(8,128)}) %reduce-scatter.28.cloned.1.call-update) | async-done | bytes 4624
  744.3 11.7 %all-reduce = bf16[96,12]{0,1:T(8,128)(2,1)S(1)} all-reduce(bf16[96,12]{0,1:T(8,128)(2,1)S(1)} %copy.206), channel_id=9, replica_groups=mesh['dp'=8,'shard'=4] {'shard'}, use_global_device_ids=true, to_apply=%region_34.35.clone | all-reduce | flops 1152 | bytes 4608
  756.6 10.8 %reduce-scatter.18.cloned.1.call-done = bf16[96,768]{1,0:T(8,128)(2,1)} async-done(((bf16[96,3072]{1,0:T(8,128)(2,1)}), bf16[96,768]{1,0:T(8,128)(2,1)}) %reduce-scatter.18.cloned.1.call-update) | async-done | bytes 147472 | tf_op jit(solution)/shard_map/reduce_scatter | solution.py:262
  767.4 1.7 fusion.87
  769.1 21.2 %reduce-scatter.16.cloned.1.call-done = bf16[96,768]{1,0:T(8,128)(2,1)} async-done(((bf16[96,3072]{1,0:T(8,128)(2,1)}), bf16[96,768]{1,0:T(8,128)(2,1)}) %reduce-scatter.16.cloned.1.call-update) | async-done | bytes 147472 | tf_op jit(solution)/shard_map/reduce_scatter | solution.py:259
  790.3 1.7 fusion.86
  793.3 20.1 %reduce-scatter.26.cloned.1.call-done = bf16[192,384]{1,0:T(8,128)(2,1)} async-done(((bf16[768,384]{1,0:T(8,128)(2,1)}), bf16[192,384]{1,0:T(8,128)(2,1)}) %reduce-scatter.26.cloned.1.call-update) | async-done | bytes 147472
  813.4 1.6 fusion.88
  816.2 1.6 copy.192
  817.8 38.6 %psum.7 = f32[]{:T(128)} all-reduce(f32[]{:T(128)S(6)} %add.274), channel_id=1, replica_groups=mesh['dp'=8,'shard'=4] {'dp','shard'}, use_global_device_ids=true, to_apply=%region_36.37 | all-reduce | flops 1 | bytes 8 | tf_op jit(solution)/shard_map/psum | solution.py:278
  857.8 2.1 multiply_add_fusion.3
  859.9 2.3 multiply_add_fusion.5
  (219 shorter events, 23.6 us)
Async XLA Ops:
  7.2 78.9 %copy-start.24 = (bf16[1024,768]{1,0:T(8,128)(2,1)S(1)}, bf16[1024,768]{1,0:T(8,128)(2,1)}, u32[]{:S(2)}) copy-start(bf16[1024,768]{1,0:T(8,128)(2,1)} %param.24) | copy-start | bytes 4718596
  7.2 80.6 %copy-start.25 = (bf16[1024,768]{1,0:T(8,128)(2,1)S(1)}, bf16[1024,768]{1,0:T(8,128)(2,1)}, u32[]{:S(2)}) copy-start(bf16[1024,768]{1,0:T(8,128)(2,1)} %param.23) | copy-start | bytes 4718596
  7.2 83.8 %all-gather.6.cloned.1.call-start = ((), (), s32[]{:S(2)}) async-start(), calls=%async_computation.7 | async-start | bytes 5308416 | tf_op jit(solution)/shard_map/all_gather | solution.py:99
  27.7 157.4 %all-gather.8.cloned.1.call-start = ((), (), s32[]{:S(2)}) async-start(), calls=%async_computation.8 | async-start | bytes 5308416 | tf_op jit(solution)/shard_map/all_gather | solution.py:100
  44.8 151.4 %all-gather.10.cloned.1.call-start = ((), (), s32[]{:S(2)}) async-start(), calls=%async_computation.9 | async-start | bytes 5308416 | tf_op jit(solution)/shard_map/all_gather | solution.py:101
  62.1 518.3 %reduce-scatter.24.cloned.1.call-start = ((), (), s32[]{:S(2)}) async-start(), calls=%async_computation.14 | async-start | bytes 10616832 | tf_op jit(solution)/shard_map/reduce_scatter | solution.py:254
  101.5 21.7 %copy-start.6 = (bf16[1024,768]{0,1:T(8,128)(2,1)}, bf16[1024,768]{0,1:T(8,128)(2,1)S(1)}, u32[]{:S(2)}) copy-start(bf16[1024,768]{0,1:T(8,128)(2,1)S(1)} %copy.179) | copy-start | bytes 4718596
  110.9 12.3 %copy-start.16 = (pred[512,1024]{1,0:T(8,128)(4,1)S(1)}, pred[512,1024]{1,0:T(8,128)(4,1)}, u32[]{:S(2)}) copy-start(pred[512,1024]{1,0:T(8,128)(4,1)} %get-tuple-element.137) | copy-start | bytes 1572868
  110.9 12.3 %copy-start.20 = (bf16[512,768]{0,1:T(8,128)(2,1)S(1)}, bf16[512,768]{0,1:T(8,128)(2,1)}, u32[]{:S(2)}) copy-start(bf16[512,768]{0,1:T(8,128)(2,1)} %copy.178) | copy-start | bytes 2359300
  123.2 11.1 %copy-start.18 = (pred[512,1024]{1,0:T(8,128)(4,1)S(1)}, pred[512,1024]{1,0:T(8,128)(4,1)}, u32[]{:S(2)}) copy-start(pred[512,1024]{1,0:T(8,128)(4,1)} %get-tuple-element.138) | copy-start | bytes 1572868
  134.3 35.0 %slice-start = ((s8[25165824]{0:T(1024)(128)(4,1)}), s8[4194304]{0:T(1024)(128)(4,1)S(1)}, s32[]{:S(2)}) async-start(s8[25165824]{0:T(1024)(128)(4,1)} %bitcast.88), calls=%async_computation.17 | async-start | bytes 8388608
  134.3 35.0 %slice-start.1 = ((s8[25165824]{0:T(1024)(128)(4,1)}), s8[4194304]{0:T(1024)(128)(4,1)S(1)}, s32[]{:S(2)}) async-start(s8[25165824]{0:T(1024)(128)(4,1)} %bitcast.88), calls=%async_computation.18 | async-start | bytes 8388608
  155.5 13.8 %slice-start.2 = ((s8[25165824]{0:T(1024)(128)(4,1)}), s8[4194304]{0:T(1024)(128)(4,1)S(1)}, s32[]{:S(2)}) async-start(s8[25165824]{0:T(1024)(128)(4,1)} %bitcast.88), calls=%async_computation.19 | async-start | bytes 8388608
  155.5 13.8 %slice-start.3 = ((s8[25165824]{0:T(1024)(128)(4,1)}), s8[4194304]{0:T(1024)(128)(4,1)S(1)}, s32[]{:S(2)}) async-start(s8[25165824]{0:T(1024)(128)(4,1)} %bitcast.88), calls=%async_computation.20 | async-start | bytes 8388608
  155.5 13.8 %slice-start.4 = ((s8[25165824]{0:T(1024)(128)(4,1)}), s8[4194304]{0:T(1024)(128)(4,1)S(1)}, s32[]{:S(2)}) async-start(s8[25165824]{0:T(1024)(128)(4,1)} %bitcast.88), calls=%async_computation.21 | async-start | bytes 8388608
  155.5 13.8 %slice-start.5 = ((s8[25165824]{0:T(1024)(128)(4,1)}), s8[4194304]{0:T(1024)(128)(4,1)S(1)}, s32[]{:S(2)}) async-start(s8[25165824]{0:T(1024)(128)(4,1)} %bitcast.88), calls=%async_computation.22 | async-start | bytes 8388608
  169.3 8.5 copy-start.35
  169.3 9.9 %copy-start.31 = (bf16[1024,768]{0,1:T(8,128)(2,1)S(1)}, bf16[1024,768]{0,1:T(8,128)(2,1)}, u32[]{:S(2)}) copy-start(bf16[1024,768]{0,1:T(8,128)(2,1)} %copy.175) | copy-start | bytes 4718596
  179.2 5.9 copy-start.38
  179.2 5.9 copy-start.39
  185.1 11.1 %copy-start.52 = (f32[3072]{0:T(1024)S(1)}, f32[3072]{0:T(1024)}, u32[]{:S(2)}) copy-start(f32[3072]{0:T(1024)} %add.249) | copy-start | bytes 36868
  185.1 11.1 %copy-start.56 = (f32[768]{0:T(1024)S(1)}, f32[768]{0:T(1024)}, u32[]{:S(2)}) copy-start(f32[768]{0:T(1024)} %get-tuple-element.106) | copy-start | bytes 9220
  196.2 14.0 %slice-start.6 = ((s8[4718592]{0:T(1024)(128)(4,1)}), s8[4194304]{0:T(1024)(128)(4,1)S(1)}, s32[]{:S(2)}) async-start(s8[4718592]{0:T(1024)(128)(4,1)} %bitcast.116), calls=%async_computation.23 | async-start | bytes 8388608
  196.2 13.2 %copy-start.5 = (bf16[1024,768]{0,1:T(8,128)(2,1)S(1)}, bf16[1024,768]{0,1:T(8,128)(2,1)}, u32[]{:S(2)}) copy-start(bf16[1024,768]{0,1:T(8,128)(2,1)} %copy.182) | copy-start | bytes 4718596
  196.2 13.2 %copy-start.49 = (f32[768]{0:T(1024)S(1)}, f32[768]{0:T(1024)}, u32[]{:S(2)}) copy-start(f32[768]{0:T(1024)} %get-tuple-element.104) | copy-start | bytes 9220
  196.2 14.0 %slice-start.7 = ((s8[4718592]{0:T(1024)(128)(4,1)}), s8[524288]{0:T(1024)(128)(4,1)S(1)}, s32[]{:S(2)}) async-start(s8[4718592]{0:T(1024)(128)(4,1)} %bitcast.116), calls=%async_computation.24 | async-start | bytes 1048576
  209.0 22.2 %copy-start.3 = (f32[1024,768]{0,1:T(8,128)}, f32[1024,768]{0,1:T(8,128)S(1)}, u32[]{:S(2)}) copy-start(f32[1024,768]{0,1:T(8,128)S(1)} %get-tuple-element.154) | copy-start | bytes 9437188
  210.3 21.0 %copy-start.1 = (f32[1024,768]{0,1:T(8,128)S(1)}, f32[1024,768]{0,1:T(8,128)}, u32[]{:S(2)}) copy-start(f32[1024,768]{0,1:T(8,128)} %copy-done) | copy-start | bytes 9437188
  241.7 384.8 %reduce-scatter.22.cloned.1.call-start = ((), (), s32[]{:S(2)}) async-start(), calls=%async_computation.13 | async-start | bytes 10616832 | tf_op jit(solution)/shard_map/reduce_scatter | solution.py:253
  241.8 14.5 %copy-start.2 = (f32[1024,768]{0,1:T(8,128)S(1)}, f32[1024,768]{0,1:T(8,128)}, u32[]{:S(2)}) copy-start(f32[1024,768]{0,1:T(8,128)} %copy-done) | copy-start | bytes 9437188
  263.6 10.5 %copy-start.7 = (bf16[1024,768]{0,1:T(8,128)(2,1)S(1)}, bf16[1024,768]{0,1:T(8,128)(2,1)}, u32[]{:S(2)}) copy-start(bf16[1024,768]{0,1:T(8,128)(2,1)} %copy-done.6) | copy-start | bytes 4718596
  338.3 51.9 %copy-start.34 = (bf16[512,12,64]{0,2,1:T(8,128)(2,1)S(1)}, bf16[512,12,64]{0,2,1:T(8,128)(2,1)}, u32[]{:S(2)}) copy-start(bf16[512,12,64]{0,2,1:T(8,128)(2,1)} %get-tuple-element.158) | copy-start | bytes 2359300
  338.3 54.3 %copy-start.21 = (bf16[512,768]{0,1:T(8,128)(2,1)S(1)}, bf16[512,768]{0,1:T(8,128)(2,1)}, u32[]{:S(2)}) copy-start(bf16[512,768]{0,1:T(8,128)(2,1)} %copy.178) | copy-start | bytes 2359300
  446.1 48.3 %copy-start.9 = (f32[1024,768]{0,1:T(8,128)S(1)}, f32[1024,768]{0,1:T(8,128)}, u32[]{:S(2)}) copy-start(f32[1024,768]{0,1:T(8,128)} %copy-done.8) | copy-start | bytes 9437188
  498.7 11.5 %copy-start.13 = (bf16[512,768]{0,1:T(8,128)(2,1)S(1)}, bf16[512,768]{0,1:T(8,128)(2,1)}, u32[]{:S(2)}) copy-start(bf16[512,768]{0,1:T(8,128)(2,1)} %copy-done.12) | copy-start | bytes 2359300
  498.7 11.5 %copy-start.17 = (pred[512,1024]{1,0:T(8,128)(4,1)S(1)}, pred[512,1024]{1,0:T(8,128)(4,1)}, u32[]{:S(2)}) copy-start(pred[512,1024]{1,0:T(8,128)(4,1)} %get-tuple-element.137) | copy-start | bytes 1572868
  510.3 14.9 %copy-start.26 = (bf16[1024,768]{1,0:T(8,128)(2,1)S(1)}, bf16[1024,768]{1,0:T(8,128)(2,1)}, u32[]{:S(2)}) copy-start(bf16[1024,768]{1,0:T(8,128)(2,1)} %param.23) | copy-start | bytes 4718596
  510.3 14.9 %copy-start.27 = (bf16[1024,12,64]{0,2,1:T(8,128)(2,1)S(1)}, bf16[1024,12,64]{0,2,1:T(8,128)(2,1)}, u32[]{:S(2)}) copy-start(bf16[1024,12,64]{0,2,1:T(8,128)(2,1)} %pad_maximum_fusion.2) | copy-start | bytes 4718596
  510.3 14.9 %copy-start.62 = (bf16[12,64,1024]{2,1,0:T(8,128)(2,1)S(1)}, bf16[12,64,1024]{2,1,0:T(8,128)(2,1)}, u32[]{:S(2)}) copy-start(bf16[12,64,1024]{2,1,0:T(8,128)(2,1)} %add_convert_fusion.1) | copy-start | bytes 4718596
  525.2 9.3 %copy-start.23 = (f32[768,768]{0,1:T(8,128)S(1)}, f32[768,768]{0,1:T(8,128)}, u32[]{:S(2)}) copy-start(f32[768,768]{0,1:T(8,128)} %fusion.74) | copy-start | bytes 7077892
  551.4 155.1 %reduce-scatter.20.cloned.1.call-start = ((), (), s32[]{:S(2)}) async-start(), calls=%async_computation.12 | async-start | bytes 10616832 | tf_op jit(solution)/shard_map/reduce_scatter | solution.py:255
  569.7 4.8 copy-start.50
  569.7 173.7 %reduce-scatter.28.cloned.1.call-start = ((), (), s32[]{:S(2)}) async-start(), calls=%async_computation.16 | async-start | bytes 442368
  577.2 51.5 %copy-start.63 = (u32[32]{0:T(128)S(1)}, u32[32]{0:T(128)}, u32[]{:S(2)}) copy-start(u32[32]{0:T(128)} %constant.85) | copy-start | bytes 388
  577.2 52.8 %copy-start.15 = (bf16[1024,768]{0,1:T(8,128)(2,1)S(1)}, bf16[1024,768]{0,1:T(8,128)(2,1)}, u32[]{:S(2)}) copy-start(bf16[1024,768]{0,1:T(8,128)(2,1)} %get-tuple-element.132) | copy-start | bytes 4718596
  579.2 52.6 %copy-start.28 = (bf16[1024,12,64]{0,2,1:T(8,128)(2,1)S(1)}, bf16[1024,12,64]{0,2,1:T(8,128)(2,1)}, u32[]{:S(2)}) copy-start(bf16[1024,12,64]{0,2,1:T(8,128)(2,1)} %pad_maximum_fusion.2) | copy-start | bytes 4718596
  580.4 187.1 %reduce-scatter.18.cloned.1.call-start = ((), (), s32[]{:S(2)}) async-start(), calls=%async_computation.11 | async-start | bytes 737280 | tf_op jit(solution)/shard_map/reduce_scatter | solution.py:262
  582.6 207.7 %reduce-scatter.16.cloned.1.call-start = ((), (), s32[]{:S(2)}) async-start(), calls=%async_computation.10 | async-start | bytes 737280 | tf_op jit(solution)/shard_map/reduce_scatter | solution.py:259
  628.7 184.6 %reduce-scatter.26.cloned.1.call-start = ((), (), s32[]{:S(2)}) async-start(), calls=%async_computation.15 | async-start | bytes 737280
  712.9 144.2 %copy-start.55 = (f32[96,3]{0,1:T(4,128)S(1)}, f32[96,3]{0,1:T(4,128)}, u32[]{:S(2)}) copy-start(f32[96,3]{0,1:T(4,128)} %param.42) | copy-start | bytes 3460
  712.9 144.2 %copy-start.59 = (f32[96,3]{0,1:T(4,128)S(1)}, f32[96,3]{0,1:T(4,128)}, u32[]{:S(2)}) copy-start(f32[96,3]{0,1:T(4,128)} %param.45) | copy-start | bytes 3460
  712.9 144.2 %copy-start.60 = (f32[96,3]{0,1:T(4,128)S(1)}, f32[96,3]{0,1:T(4,128)}, u32[]{:S(2)}) copy-start(f32[96,3]{0,1:T(4,128)} %param.44) | copy-start | bytes 3460
  712.9 144.2 %copy-start.61 = (f32[96,3]{0,1:T(4,128)S(1)}, f32[96,3]{0,1:T(4,128)}, u32[]{:S(2)}) copy-start(f32[96,3]{0,1:T(4,128)} %param.43) | copy-start | bytes 3460
  713.0 144.8 %copy-start.40 = (f32[384,192]{0,1:T(8,128)S(1)}, f32[384,192]{0,1:T(8,128)}, u32[]{:S(2)}) copy-start(f32[384,192]{0,1:T(8,128)} %param.41) | copy-start | bytes 884740
  713.0 144.8 %copy-start.41 = (f32[384,192]{0,1:T(8,128)S(1)}, f32[384,192]{0,1:T(8,128)}, u32[]{:S(2)}) copy-start(f32[384,192]{0,1:T(8,128)} %param.38) | copy-start | bytes 884740
  713.0 144.8 %copy-start.42 = (f32[384,192]{0,1:T(8,128)S(1)}, f32[384,192]{0,1:T(8,128)}, u32[]{:S(2)}) copy-start(f32[384,192]{0,1:T(8,128)} %param.40) | copy-start | bytes 884740
  713.0 144.8 %copy-start.43 = (f32[384,192]{0,1:T(8,128)S(1)}, f32[384,192]{0,1:T(8,128)}, u32[]{:S(2)}) copy-start(f32[384,192]{0,1:T(8,128)} %param.39) | copy-start | bytes 884740
  717.8 142.1 %copy-start.44 = (f32[96,768]{1,0:T(8,128)S(1)}, f32[96,768]{1,0:T(8,128)}, u32[]{:S(2)}) copy-start(f32[96,768]{1,0:T(8,128)} %param.33) | copy-start | bytes 884740
  767.4 94.8 %copy-start.36 = (bf16[96,768]{1,0:T(8,128)(2,1)S(1)}, bf16[96,768]{1,0:T(8,128)(2,1)}, u32[]{:S(2)}) copy-start(bf16[96,768]{1,0:T(8,128)(2,1)} %reduce-scatter.18.cloned.1.call-done) | copy-start | bytes 442372
  790.3 69.6 %copy-start.37 = (bf16[96,768]{1,0:T(8,128)(2,1)S(1)}, bf16[96,768]{1,0:T(8,128)(2,1)}, u32[]{:S(2)}) copy-start(bf16[96,768]{1,0:T(8,128)(2,1)} %reduce-scatter.16.cloned.1.call-done) | copy-start | bytes 442372
  817.8 44.4 %copy-start.45 = (f32[96,768]{1,0:T(8,128)S(1)}, f32[96,768]{1,0:T(8,128)}, u32[]{:S(2)}) copy-start(f32[96,768]{1,0:T(8,128)} %param.37) | copy-start | bytes 884740
  817.8 44.4 %copy-start.46 = (f32[96,768]{1,0:T(8,128)S(1)}, f32[96,768]{1,0:T(8,128)}, u32[]{:S(2)}) copy-start(f32[96,768]{1,0:T(8,128)} %param.34) | copy-start | bytes 884740
  817.8 44.4 %copy-start.47 = (f32[96,768]{1,0:T(8,128)S(1)}, f32[96,768]{1,0:T(8,128)}, u32[]{:S(2)}) copy-start(f32[96,768]{1,0:T(8,128)} %param.36) | copy-start | bytes 884740
  817.8 44.4 %copy-start.48 = (f32[96,768]{1,0:T(8,128)S(1)}, f32[96,768]{1,0:T(8,128)}, u32[]{:S(2)}) copy-start(f32[96,768]{1,0:T(8,128)} %param.35) | copy-start | bytes 884740
  (18 other events, 59.3 us)
Sparse Core Ops, SparseCore 0:
  27.8 38.3 all-gather.5
  68.1 38.9 all-gather.7
  109.0 39.7 all-gather.9
  241.8 74.6 reduce-scatter.23
  551.5 75.0 reduce-scatter.21
  629.9 76.4 reduce-scatter.19
  709.5 33.8 reduce-scatter.27
  745.7 21.6 reduce-scatter.17
  769.7 20.5 reduce-scatter.15
  793.0 20.2 reduce-scatter.25
where the time goes:
time: 882 us; the launch traced here: 872 us
  matrix products  425 us (48%)
  waiting for transfers between devices  192 us (22%)
  blocking collectives  124 us (14%)
  other arithmetic  69.1 us (8%)
  local copies, waits for them, and re-layouts  40.3 us (5%)
  between operations  21.3 us (2%)
    dot_general x2, matrix products, on_device(): jnp.einsum('hqk,khd->qhd', d_scores, k_heads, preferred_element_type=jnp....  104 us
    dot_general x2, matrix products, on_device(): jnp.einsum('hqk,qhd->khd', d_scores, q_part, preferred_element_type=jnp.f...  102 us
    reduce_scatter x1, waiting for transfers between devices, on_device(): lax.psum_scatter(grad_down, 'dp', scatter_dimension=0, tiled=True)  70.2 us
    dot_general x6, matrix products, contract_last(): lax.dot_general(left, right, (((1,), (1,)), ((), ())), preferred_element_...  51.6 us
    unnamed x12, waiting for transfers between devices  45.8 us
    reduce_scatter x1, waiting for transfers between devices, on_device(): lax.psum_scatter(grad_attn, 'dp', scatter_dimension=0, tiled=True)  43.9 us
    psum x1, blocking collectives, on_device(): grad_norm = jnp.sqrt(lax.psum(local_squares, ('dp', 'shard')))  38.6 us
    unnamed x154, local copies, waits for them, and re-layouts  30.4 us
  transfers between devices with their start and end apart: 10, of which 6 were waited for; matrix products, arithmetic and copies ran while one was open for 54% of the time, Pallas kernels for 0%

commit v1 on v0

v1 whole, which is shorter than its diff:
```python
import functools
import math

import jax
import jax.numpy as jnp
from jax import lax
from jax.experimental import pallas as pl
from jax.experimental.pallas import tpu as pltpu
from jax.sharding import PartitionSpec as P

HEAD_DIM = 64
STEP = 10

norm_eps = 1e-06
clip_limit = 1.0
beta_first = 0.9
beta_second = 0.999
adam_eps = 1e-08
matrix_rate = 0.08
vector_rate = 0.5
matrix_decay = 0.01
average_keep = 0.9

VMEM = 58 * 2**20
GELU_K = math.sqrt(2.0 / math.pi)
GELU_C = 0.044715
f32 = jnp.float32
bf16 = jnp.bfloat16
SDS = jax.ShapeDtypeStruct


def dot(left, right):
    return jnp.dot(left, right, preferred_element_type=f32)


def dot_last(left, right):
    return lax.dot_general(left, right, (((1,), (1,)), ((), ())), preferred_element_type=f32)


def col_sum(value):
    return jnp.sum(value, axis=0, keepdims=True)


def params(**extra):
    return pltpu.CompilerParams(vmem_limit_bytes=VMEM, **extra)


def cost(flops, moved, trans=0):
    return pl.CostEstimate(flops=int(flops), bytes_accessed=int(moved), transcendentals=int(trans))


SMEM = pl.BlockSpec(memory_space=pltpu.SMEM)


def normalize(value):
    centre = value - jnp.mean(value, axis=-1, keepdims=True)
    inv_std = lax.rsqrt(jnp.mean(centre * centre, axis=-1, keepdims=True) + norm_eps)
    return centre * inv_std, inv_std


def normalize_back(scaled, normed, inv_std):
    return inv_std * (
        scaled
        - jnp.mean(scaled, axis=-1, keepdims=True)
        - normed * jnp.mean(scaled * normed, axis=-1, keepdims=True)
    )


def attn_fwd_kernel(
    len_ref, scale_ref, x_ref, wq_ref, wk_ref, wv_ref, bq_ref, bv_ref,
    q_ref, k_ref, v_ref, c_ref, lse_ref, *, block,
):
    rows, width = q_ref.shape
    x = x_ref[...]
    q_ref[...] = (dot(x, wq_ref[...]) * scale_ref[0] + bq_ref[...]).astype(bf16)
    k_ref[...] = (dot(x, wk_ref[...]) * scale_ref[1]).astype(bf16)
    v_ref[...] = (dot(x, wv_ref[...]) * scale_ref[2] + bv_ref[...]).astype(bf16)
    lane = lax.broadcasted_iota(jnp.int32, (1, 128), 1)

    def run(span):
        step = min(block, span)
        for pair in range(width // 128):
            cols = pl.ds(pair * 128, 128)
            for start in range(0, rows, step):
                low = start // span * span
                q_rows = q_ref[start : start + step, cols]
                k_rows = k_ref[low : low + span, cols]
                v_rows = v_ref[low : low + span, cols]
                found = []
                for head in range(2):
                    own = (lane < 64) if head == 0 else (lane >= 64)
                    q_own = jnp.where(own, q_rows, jnp.zeros_like(q_rows)) * jnp.asarray(0.125, bf16)
                    v_ones = jnp.where(own, v_rows, jnp.ones_like(v_rows))
                    scores = dot_last(q_own, k_rows)
                    top = jnp.max(scores, axis=1, keepdims=True)
                    found.append((dot(jnp.exp(scores - top).astype(bf16), v_ones), top))
                (out_a, top_a), (out_b, top_b) = found
                value = jnp.where(lane < 64, out_a, out_b)
                total = jnp.where(lane < 64, pltpu.roll(out_a, 64, 1), pltpu.roll(out_b, 64, 1))
                c_ref[start : start + step, cols] = (value / total).astype(bf16)
                lse_ref[start : start + step, cols] = jnp.where(lane < 64, top_a, top_b) + jnp.log(total)

    two = len_ref[0] < rows

    @pl.when(two)
    def _():
        run(rows // 2)

    @pl.when(jnp.logical_not(two))
    def _():
        run(rows)


def attn_fwd(lengths, scales, x, w_attn, bias_q, bias_v):
    rows, width = x.shape
    group = 256
    count = width // group

    def cols(height, part=0):
        return pl.BlockSpec((height, group), lambda g: (0, part * count + g))

    return pl.pallas_call(
        functools.partial(attn_fwd_kernel, block=512),
        grid=(count,),
        in_specs=[SMEM, SMEM, pl.BlockSpec((rows, width), lambda g: (0, 0)),
                  cols(width, 0), cols(width, 1), cols(width, 2), cols(1), cols(1)],
        out_specs=[cols(rows)] * 5,
        out_shape=[SDS((rows, width), bf16)] * 4 + [SDS((rows, width), f32)],
        compiler_params=params(),
        cost_estimate=cost(20e9, 12e6, 12e6),
        name="attention_forward",
    )(lengths, scales, x, w_attn, w_attn, w_attn, bias_q, bias_v)


def attn_bwd_kernel(
    len_ref, q_ref, k_ref, v_ref, dc_ref, c_ref, lse_ref,
    dq_ref, dk_ref, dv_ref, sum_q_ref, sum_v_ref, dk_acc, dv_acc, dq_acc, *, block,
):
    rows = q_ref.shape[0]
    lane = lax.broadcasted_iota(jnp.int32, (1, 128), 1)
    masks = [lane < 64, lane >= 64]
    prod = (dc_ref[...].astype(f32) * c_ref[...].astype(f32)).T
    row_dots = [col_sum(prod[:64]), col_sum(prod[64:])]
    lse = lse_ref[...].T
    lse_rows = [lse[0:1], lse[64:65]]

    def run(span):
        step = min(block, span)
        for low in range(0, rows, span):
            k_rows = k_ref[low : low + span, :]
            v_rows = v_ref[low : low + span, :]
            k_cols = k_rows.astype(f32).T.astype(bf16)
            for start in range(low, low + span, step):
                q_rows = q_ref[start : start + step, :]
                dc_rows = dc_ref[start : start + step, :]
                probs, d_scores, q_own, dc_own, dq_parts = [], [], [], [], []
                for head in range(2):
                    q_head = jnp.where(masks[head], q_rows, jnp.zeros_like(q_rows)) * jnp.asarray(0.125, bf16)
                    dc_head = jnp.where(masks[head], dc_rows, jnp.zeros_like(dc_rows))
                    prob = jnp.exp(dot_last(k_rows, q_head) - lse_rows[head][:, start : start + step])
                    d_prob = dot_last(v_rows, dc_head)
                    d_score = (prob * (d_prob - row_dots[head][:, start : start + step])).astype(bf16)
                    probs.append(prob.astype(bf16))
                    d_scores.append(d_score)
                    q_own.append(q_head)
                    dc_own.append(dc_head)
                    dq_parts.append(dot(k_cols[head * 64 : head * 64 + 64], d_score))
                dq_acc[:, start : start + step] = jnp.concatenate(dq_parts, axis=0)
                dv = dot(jnp.concatenate(probs, axis=1), jnp.concatenate(dc_own, axis=0))
                dk = dot(jnp.concatenate(d_scores, axis=1), jnp.concatenate(q_own, axis=0))
                if start == low:
                    dv_acc[low : low + span, :] = dv
                    dk_acc[low : low + span, :] = dk
                else:
                    dv_acc[low : low + span, :] += dv
                    dk_acc[low : low + span, :] += dk

    two = len_ref[0] < rows

    @pl.when(two)
    def _():
        run(rows // 2)

    @pl.when(jnp.logical_not(two))
    def _():
        run(rows)

    dq = dq_acc[...].T * 0.125
    dq_ref[...] = dq.astype(bf16)
    dk_ref[...] = dk_acc[...].astype(bf16)
    dv_ref[...] = dv_acc[...].astype(bf16)
    sum_q_ref[...] = jnp.broadcast_to(col_sum(dq), sum_q_ref.shape)
    sum_v_ref[...] = jnp.broadcast_to(col_sum(dv_acc[...]), sum_v_ref.shape)


def attn_bwd(lengths, q, k, v, dc, c, lse):
    rows, width = q.shape
    cols = pl.BlockSpec((rows, 128), lambda g: (0, g))
    sums = pl.BlockSpec((8, 128), lambda g: (0, g))
    return pl.pallas_call(
        functools.partial(attn_bwd_kernel, block=512),
        grid=(width // 128,),
        in_specs=[SMEM] + [cols] * 6,
        out_specs=[cols] * 3 + [sums] * 2,
        out_shape=[SDS((rows, width), bf16)] * 3 + [SDS((8, width), f32)] * 2,
        scratch_shapes=[pltpu.VMEM((rows, 128), f32), pltpu.VMEM((rows, 128), f32), pltpu.VMEM((128, rows), f32)],
        compiler_params=params(),
        cost_estimate=cost(40e9, 20e6, 12e6),
        name="attention_backward",
    )(lengths, q, k, v, dc, c, lse)


def mid_fwd_kernel(scale_ref, x_ref, c_ref, wo_ref, w1_ref, vec_ref, b1_ref, n1_ref, r1_ref, y1_ref, a_ref, gp_ref, *, chunk):
    rows = x_ref.shape[0]
    residual = x_ref[...].astype(f32) + dot(c_ref[...], wo_ref[...]) * scale_ref[3] + vec_ref[2:3]
    normed, inv_std = normalize(residual)
    n1_ref[...] = normed
    r1_ref[...] = jnp.broadcast_to(inv_std, (rows, 128))
    y1 = (normed * vec_ref[3:4] + vec_ref[4:5]).astype(bf16)
    y1_ref[...] = y1
    for start in range(0, w1_ref.shape[1], chunk):
        cols = slice(start, start + chunk)
        u = dot(y1, w1_ref[:, cols]) * scale_ref[4] + b1_ref[:, cols]
        square = u * u
        half = 0.5 + 0.5 * jnp.tanh(u * (GELU_K + (GELU_K * GELU_C) * square))
        act = u * half
        a_ref[:, cols] = act.astype(bf16)
        gp_ref[:, cols] = (half + act * (1.0 - half) * (2 * GELU_K + (6 * GELU_K * GELU_C) * square)).astype(bf16)


def mid_fwd(scales, x, c, w_out, w_up, vec, bias_up):
    rows, width = x.shape
    hidden = w_up.shape[1]
    tile = 512

    def row(size):
        return pl.BlockSpec((tile, size), lambda i: (i, 0))

    def full(arr):
        return pl.BlockSpec(arr.shape, lambda i: (0, 0))

    return pl.pallas_call(
        functools.partial(mid_fwd_kernel, chunk=256),
        grid=(rows // tile,),
        in_specs=[SMEM, row(width), row(width), full(w_out), full(w_up), full(vec), full(bias_up)],
        out_specs=[row(width), row(128), row(width), row(hidden), row(hidden)],
        out_shape=[SDS((rows, width), f32), SDS((rows, 128), f32), SDS((rows, width), bf16),
                   SDS((rows, hidden), bf16), SDS((rows, hidden), bf16)],
        compiler_params=params(),
        cost_estimate=cost(12e9, 25e6, 3e6),
        name="middle_forward",
    )(scales, x, c, w_out, w_up, vec, bias_up)


def mid_bwd_kernel(
    scale_ref, n1_ref, r1_ref, a_ref, gp_ref, do_ref, w2_ref, w1_ref, wo_ref, vec_ref,
    out_ref, dz_ref, du_ref, dh_ref, dhb_ref, dc_ref, vg_ref, b1g_ref, *, chunk,
):
    @pl.when(pl.program_id(0) == 0)
    def _():
        vg_ref[...] = jnp.zeros_like(vg_ref)
        b1g_ref[...] = jnp.zeros_like(b1g_ref)

    g1, c1, b2, g2, c2 = [vec_ref[i : i + 1] for i in range(3, 8)]
    n1 = n1_ref[...]
    residual = n1 * g1 + c1 + dot_last(a_ref[...], w2_ref[...]) * scale_ref[5] + b2
    n2, r2 = normalize(residual)
    out_ref[...] = (n2 * g2 + c2).astype(bf16)
    d_out = do_ref[...].astype(f32)
    vg_ref[6:7] += col_sum(d_out * n2)
    vg_ref[7:8] += col_sum(d_out)
    dz = normalize_back(d_out * g2, n2, r2)
    vg_ref[5:6] += col_sum(dz)
    dz_low = dz.astype(bf16)
    dz_ref[...] = dz_low
    for start in range(0, w1_ref.shape[1], chunk):
        cols = slice(start, start + chunk)
        du = dot(dz_low, w2_ref[:, cols]) * scale_ref[5] * gp_ref[:, cols].astype(f32)
        b1g_ref[0:1, cols] += col_sum(du)
        du_ref[:, cols] = du.astype(bf16)
    dy = dz + dot_last(du_ref[...], w1_ref[...]) * scale_ref[4]
    vg_ref[3:4] += col_sum(dy * n1)
    vg_ref[4:5] += col_sum(dy)
    dh = normalize_back(dy * g1, n1, r1_ref[:, 0:1])
    vg_ref[2:3] += col_sum(dh)
    dh_ref[...] = dh
    dh_low = dh.astype(bf16)
    dhb_ref[...] = dh_low
    dc_ref[...] = (dot_last(dh_low, wo_ref[...]) * scale_ref[3]).astype(bf16)


def mid_bwd(scales, n1, r1, act, gelu_grad, d_out, w_down_t, w_up, w_out, vec):
    rows, width = n1.shape
    hidden = w_up.shape[1]
    tile = 256

    def row(size):
        return pl.BlockSpec((tile, size), lambda i: (i, 0))

    def full(arr):
        return pl.BlockSpec(arr.shape, lambda i: (0, 0))

    return pl.pallas_call(
        functools.partial(mid_bwd_kernel, chunk=256),
        grid=(rows // tile,),
        in_specs=[SMEM, row(width), row(128), row(hidden), row(hidden), row(width),
                  full(w_down_t), full(w_up), full(w_out), full(vec)],
        out_specs=[row(width), row(width), row(hidden), row(width), row(width), row(width),
                   pl.BlockSpec((8, width), lambda i: (0, 0)), pl.BlockSpec((8, hidden), lambda i: (0, 0))],
        out_shape=[SDS((rows, width), bf16), SDS((rows, width), bf16), SDS((rows, hidden), bf16),
                   SDS((rows, width), f32), SDS((rows, width), bf16), SDS((rows, width), bf16),
                   SDS((8, width), f32), SDS((8, hidden), f32)],
        compiler_params=params(),
        cost_estimate=cost(25e9, 45e6),
        name="middle_backward",
    )(scales, n1, r1, act, gelu_grad, d_out, w_down_t, w_up, w_out, vec)


def weight_grad_kernel(left_ref, *refs, count):
    right, outs, left_t = refs[:count], refs[count : 2 * count], refs[2 * count]

    @pl.when(pl.program_id(0) == 0)
    def _():
        left_t[...] = left_ref[...].T

    for r, o in zip(right, outs):
        o[...] = dot(left_t[...], r[...]).astype(bf16)


def weight_grad(left, rights, chunk):
    rows, width = left.shape
    size = rights[0].shape[1]
    count = len(rights)
    return pl.pallas_call(
        functools.partial(weight_grad_kernel, count=count),
        grid=(size // chunk,),
        in_specs=[pl.BlockSpec((rows, width), lambda i: (0, 0))]
        + [pl.BlockSpec((rows, chunk), lambda i: (0, i))] * count,
        out_specs=[pl.BlockSpec((width, chunk), lambda i: (0, i))] * count,
        out_shape=[SDS((width, size), bf16)] * count,
        scratch_shapes=[pltpu.VMEM((width, rows), bf16)],
        compiler_params=params(),
        cost_estimate=cost(3 * rows * width * size * count, 2 * (rows * width + count * size * (rows + width))),
        name="weight_gradient",
    )(left, *rights)


def input_grad_kernel(scale_ref, dh_ref, dq_ref, dk_ref, dv_ref, wq_ref, wk_ref, wv_ref, out_ref):
    total = dh_ref[...] + dot_last(dq_ref[...], wq_ref[...]) * scale_ref[0]
    total = total + dot_last(dk_ref[...], wk_ref[...]) * scale_ref[1]
    out_ref[...] = (total + dot_last(dv_ref[...], wv_ref[...]) * scale_ref[2]).astype(bf16)


def input_grad(scales, dh, dq, dk, dv, w_attn):
    rows, width = dh.shape
    tile = 512
    row = pl.BlockSpec((tile, width), lambda i: (i, 0))

    def part(index):
        return pl.BlockSpec((width, width), lambda i: (0, index))

    return pl.pallas_call(
        input_grad_kernel,
        grid=(rows // tile,),
        in_specs=[SMEM] + [row] * 4 + [part(i) for i in range(3)],
        out_specs=row,
        out_shape=SDS((rows, width), bf16),
        compiler_params=params(),
        cost_estimate=cost(9e9, 2 * (rows * width * 6 + 3 * width * width)),
        name="input_gradient",
    )(scales, dh, dq, dk, dv, w_attn, w_attn, w_attn)


def adam_update(gradient, master, first_old, second_old, average, step_rate, decay_rate):
    first_new = beta_first * first_old + (1.0 - beta_first) * gradient
    second_new = beta_second * second_old + (1.0 - beta_second) * gradient * gradient
    first_hat = first_new / (1.0 - beta_first**STEP)
    second_hat = second_new / (1.0 - beta_second**STEP)
    master_new = master - step_rate * (
        first_hat / (jnp.sqrt(second_hat) + adam_eps) + decay_rate * master
    )
    average_new = average_keep * average + (1.0 - average_keep) * master_new
    return (first_new, second_new, master_new, average_new)


def on_device(
    tokens, out_grad, first_lengths, quant_scales, attn_quant, up_quant, down_quant,
    attn_master, attn_first, attn_second, attn_average,
    up_master, up_first, up_second, up_average,
    down_master, down_first, down_second, down_average,
    vector_master, vector_first, vector_second, vector_average,
):
    width = tokens.shape[1]
    gather = functools.partial(lax.all_gather, tiled=True)
    scatter = functools.partial(lax.psum_scatter, tiled=True)
    vector_low = vector_master.astype(bf16)
    attn_w = gather(gather(attn_quant, "shard", axis=1), "dp", axis=0)
    vec_w = gather(gather(vector_low, "shard", axis=1), "dp", axis=0)
    up_w = gather(gather(up_quant, "shard", axis=1), "dp", axis=0)
    down_t = gather(gather(down_quant.T, "shard", axis=0), "dp", axis=1)
    vec = vec_w.astype(f32).T
    bias_up = vec[8:].reshape(1, -1)
    vec = vec[:8]

    q, k, v, c, lse = attn_fwd(first_lengths, quant_scales, tokens, attn_w, vec[0:1], vec[1:2])
    w_out = attn_w[:, 3 * width :]
    n1, r1, y1, act, gelu_grad = mid_fwd(quant_scales, tokens, c, w_out, up_w, vec, bias_up)
    layer_out, dz, du, dh, dh_low, dc, vec_grad, b1_grad = mid_bwd(
        quant_scales, n1, r1, act, gelu_grad, out_grad, down_t, up_w, w_out, vec
    )
    (grad_down_t,) = weight_grad(dz, [act], 768)
    (grad_up,) = weight_grad(y1, [du], 768)
    (grad_out_proj,) = weight_grad(c, [dh_low], 768)
    dq, dk, dv, sum_q, sum_v = attn_bwd(first_lengths, q, k, v, dc, c, lse)
    grad_qkv = weight_grad(tokens, [dq, dk, dv], 256)
    input_gradient = input_grad(quant_scales, dh, dq, dk, dv, attn_w)

    vec_rows = jnp.concatenate([sum_q[0:1], sum_v[0:1], vec_grad[2:8], b1_grad[0:1].reshape(-1, width)], axis=0)
    own_down = scatter(scatter(grad_down_t, "dp", scatter_dimension=1), "shard", scatter_dimension=0)
    own_up = scatter(scatter(grad_up, "dp", scatter_dimension=0), "shard", scatter_dimension=1)
    grad_attn = jnp.concatenate(list(grad_qkv) + [grad_out_proj], axis=1)
    own_attn = scatter(scatter(grad_attn, "dp", scatter_dimension=0), "shard", scatter_dimension=1)
    own_vector = scatter(scatter(vec_rows.T, "dp", scatter_dimension=0), "shard", scatter_dimension=1)
    own_down = own_down.astype(f32).T
    own_up = own_up.astype(f32)
    own_attn = own_attn.astype(f32)
    local_squares = (
        jnp.sum(own_attn * own_attn)
        + jnp.sum(own_up * own_up)
        + jnp.sum(own_down * own_down)
        + jnp.sum(own_vector * own_vector)
    )
    grad_norm = jnp.sqrt(lax.psum(local_squares, ("dp", "shard")))
    factor = jnp.minimum(1.0, clip_limit / (grad_norm + norm_eps))
    attn_new = adam_update(own_attn * factor, attn_master, attn_first, attn_second, attn_average, matrix_rate, matrix_decay)
    up_new = adam_update(own_up * factor, up_master, up_first, up_second, up_average, matrix_rate, matrix_decay)
    down_new = adam_update(own_down * factor, down_master, down_first, down_second, down_average, matrix_rate, matrix_decay)
    vector_new = adam_update(own_vector * factor, vector_master, vector_first, vector_second, vector_average, vector_rate, 0.0)
    return (layer_out, input_gradient, grad_norm, *attn_new, *up_new, *down_new, *vector_new)


def solution(mesh):
    rows = P(("dp", "shard"), None)
    block = P("dp", "shard")
    in_specs = (rows, rows, P(("dp", "shard")), P()) + (block,) * 19
    out_specs = (rows, rows, P()) + (block,) * 16
    return jax.shard_map(
        on_device, mesh=mesh, in_specs=in_specs, out_specs=out_specs, check_vma=False
    )
```

time: 882 us -> 585 us (0.66)
  matrix products: 425 us -> 0 us
  Pallas kernels: 0 us -> 154 us
  other arithmetic: 69.1 us -> 14.8 us
  waiting for transfers between devices: 192 us -> 244 us
  local copies, waits for them, and re-layouts: 40.3 us -> 18.1 us
    dot_general x25 -> x0, matrix products: 414 us -> none  [the longest x2 104 us: on_device(): jnp.einsum('hqk,khd->qhd', d_scores, k_heads, preferred_element_type=jnp....]
    pallas_call x0 -> x9, Pallas kernels: none -> 154 us  [the longest x1 38.3 us: attn_bwd(): pl.pallas_call(functools.partial(attn_bwd_kernel, block=512), grid=(width...]
    unnamed x12, waiting for transfers between devices: 45.8 us -> 91.1 us
    reduce_sum x10 -> x0, other arithmetic: 33.2 us -> none  [the longest x1 21.2 us: on_device(): row_total = jnp.sum(exponent, axis=-1, keepdims=True)]
    all_gather x3, waiting for transfers between devices: 0.02 us -> 19.1 us  [the longest x1 19.1 us: on_device(): down_t = gather(gather(down_quant.T, 'shard', axis=0), 'dp', axis=1)]
    unnamed x154 -> x48, local copies, waits for them, and re-layouts: 30.4 us -> 11.9 us
    reduce_scatter x5, waiting for transfers between devices: 146 us -> 134 us  [the longest x1 57.5 us: on_device(): scatter(grad_up, 'dp', scatter_dimension=0)]
    convert_element_type x6 -> x0, other arithmetic: 10.8 us -> none  [the longest x1 5.14 us: on_device(): queries = (qkv_raw[:, :model_width] + bias_q).astype(jnp.bfloat16)]
  transfers between devices with their start and end apart: 10 -> 10, of which waited for: 6 -> 8; matrix products, arithmetic and copies ran while one was open for 54% -> 4% of each run, Pallas kernels for 0% -> 11%
where the time goes in v1:
time: 585 us; the launch traced here: 576 us
  waiting for transfers between devices  244 us (42%)
  Pallas kernels  154 us (26%)
  blocking collectives  124 us (21%)
  between operations  20.7 us (4%)
  local copies, waits for them, and re-layouts  18.1 us (3%)
  other arithmetic  14.8 us (3%)
    unnamed x12, waiting for transfers between devices  91.1 us
    reduce_scatter x1, waiting for transfers between devices, on_device(): scatter(grad_up, 'dp', scatter_dimension=0)  57.5 us
    psum x1, blocking collectives, on_device(): grad_norm = jnp.sqrt(lax.psum(local_squares, ('dp', 'shard')))  38.5 us
    pallas_call x1, Pallas kernels, attn_bwd(): pl.pallas_call(functools.partial(attn_bwd_kernel, block=512), grid=(width...  38.3 us
    pallas_call x4, Pallas kernels, weight_grad(): pl.pallas_call(functools.partial(weight_grad_kernel, count=count), grid=(...  32.5 us
    pallas_call x1, Pallas kernels, mid_bwd(): pl.pallas_call(functools.partial(mid_bwd_kernel, chunk=256), grid=(rows /...  31.2 us
    pallas_call x1, Pallas kernels, attn_fwd(): pl.pallas_call(functools.partial(attn_fwd_kernel, block=512), grid=(count...  25 us
    reduce_scatter x1, waiting for transfers between devices, on_device(): scatter(grad_attn, 'dp', scatter_dimension=0)  23.8 us
  transfers between devices with their start and end apart: 10, of which 8 were waited for; matrix products, arithmetic and copies ran while one was open for 4% of the time, Pallas kernels for 11%

profile of v1, /device:TPU:0, one launch (start us, length us, event | category | flops | bytes accessed | tf_op | source)
XLA Modules:
  0.0 576.0 jit_solution(11763769720283624974)
XLA Ops:
  7.2 0.0 all-gather.6.cloned.1.call-start
  7.2 20.2 %all_gather.24 = bf16[96,3072]{1,0:T(8,128)(2,1)} all-gather(bf16[96,768]{1,0:T(8,128)(2,1)} %param.27), channel_id=1, replica_groups=mesh['dp'=8,'shard'=4] {'shard'}, dimensions={1}, use_global_device_ids=true | all-gather | bytes 737280 | tf_op jit(solution)/shard_map/all_gather | solution.py:397
  27.4 0.0 all-gather.6.cloned.1.call-update
  27.4 0.0 all-gather.8.cloned.1.call-start
  27.5 16.7 %all_gather.28 = bf16[96,3072]{1,0:T(8,128)(2,1)} all-gather(bf16[96,768]{1,0:T(8,128)(2,1)} %param.28), channel_id=1, replica_groups=mesh['dp'=8,'shard'=4] {'shard'}, dimensions={1}, use_global_device_ids=true | all-gather | bytes 737280 | tf_op jit(solution)/shard_map/all_gather | solution.py:399
  44.2 0.0 all-gather.8.cloned.1.call-update
  44.2 0.0 all-gather.10.cloned.1.call-start
  44.3 17.0 %all_gather.30 = bf16[768,384]{1,0:T(8,128)(2,1)} all-gather(bf16[192,384]{1,0:T(8,128)(2,1)} %bitcast.38), channel_id=1, replica_groups=mesh['dp'=8,'shard'=4] {'shard'}, dimensions={0}, use_global_device_ids=true | all-gather | bytes 737280 | tf_op jit(solution)/shard_map/all_gather | solution.py:400
  61.3 0.0 all-gather.10.cloned.1.call-update
  61.3 0.0 reduce-scatter.12.cloned.1.call-start
  61.4 10.2 %all-gather = bf16[4,3,96]{2,1,0:T(4,128)(2,1)S(1)} all-gather(bf16[1,3,96]{2,1,0:T(4,128)(2,1)S(1)} %convert_bitcast_fusion), channel_id=1, replica_groups=mesh['dp'=8,'shard'=4] {'shard'}, dimensions={0}, use_global_device_ids=true | all-gather | bytes 2880 | tf_op jit(solution)/shard_map/all_gather | solution.py:398
  71.6 9.1 %all-gather.1 = bf16[8,96,12]{1,2,0:T(8,128)(2,1)S(1)} all-gather(bf16[1,96,12]{1,2,0:T(8,128)(2,1)S(1)} %bitcast.39), channel_id=1, replica_groups=mesh['dp'=8,'shard'=4] {'dp'}, dimensions={0}, use_global_device_ids=true | all-gather | bytes 20736 | tf_op jit(solution)/shard_map/all_gather | solution.py:398
  80.7 0.1 reshape.50
  81.5 0.6 slice.41.vec_ref
  82.1 0.6 copy.49
  82.7 0.6 fusion.21
  83.3 2.4 slice.40.wo_ref
  85.7 25.0 %attention_forward.1 = (bf16[1024,768]{1,0:T(8,128)(2,1)}, bf16[1024,768]{1,0:T(8,128)(2,1)}, bf16[1024,768]{1,0:T(8,128)(2,1)}, bf16[1024,768]{1,0:T(8,128)(2,1)}, f32[1024,768]{1,0:T(8,128)}) custom-call(s32[1]{0:T(128)S(6)} %copy.51.len_ref, f32[6]{0:T(128)} %scale_ref.7, bf16[1024,768]{1,0:T(8,128)(2,1)} %left_ref.1, ...), custom_call_target="tpu_custom_call" | custom-call | flops 20000000000 | bytes 12000000 | tf_op jit(solution)/shard_map/attention_forward/pallas_call | solution.py:122
  110.8 18.9 %middle_forward.1 = (f32[1024,768]{1,0:T(8,128)}, f32[1024,128]{1,0:T(8,128)}, bf16[1024,768]{1,0:T(8,128)(2,1)}, bf16[1024,3072]{1,0:T(8,128)(2,1)}, bf16[1024,3072]{1,0:T(8,128)(2,1)}) custom-call(f32[6]{0:T(128)} %scale_ref.7, bf16[1024,768]{1,0:T(8,128)(2,1)} %left_ref.1, bf16[1024,768]{1,0:T(8,128)(2,1)} %get-tuple-element.45.c_ref.left_ref, ...), custom_call_target="tpu_custom_call" | custom-call | flops 12000000000 | bytes 25000000 | tf_op jit(solution)/shard_map/middle_forward/pallas_call | solution.py:242
  129.6 19.1 %all-gather.10.cloned.1.call-done.w2_ref = bf16[768,3072]{1,0:T(8,128)(2,1)} async-done(((bf16[768,384]{1,0:T(8,128)(2,1)}), bf16[768,3072]{1,0:T(8,128)(2,1)}) %all-gather.10.cloned.1.call-update) | async-done | bytes 4718608 | tf_op jit(solution)/shard_map/all_gather | solution.py:400
  148.7 31.2 %middle_backward.1 = (bf16[1024,768]{1,0:T(8,128)(2,1)}, bf16[1024,768]{1,0:T(8,128)(2,1)}, bf16[1024,3072]{1,0:T(8,128)(2,1)}, f32[1024,768]{1,0:T(8,128)}, bf1...) custom-call(f32[6]{0:T(128)} %scale_ref.7, ...), custom_call_target="tpu_custom_call" | custom-call | flops 24999999488 | bytes 45000000 | tf_op jit(solution)/shard_map/middle_backward/pallas_call | solution.py:303
  179.9 4.4 weight_gradient.5
  184.2 38.3 %attention_backward.1 = (bf16[1024,768]{1,0:T(8,128)(2,1)}, bf16[1024,768]{1,0:T(8,128)(2,1)}, bf16[1024,768]{1,0:T(8,128)(2,1)}, f32[8,768]{1,0:T(8,128)}, f32[8,768]{1,0:T(8,128)}) custom-call(s32[1]{0:T(128)S(6)} %copy.51.len_ref, bf16[1024,768]{1,0:T(8,128)(2,1)} %get-tuple-element.52.q_ref, bf16[1024,768]{1,0:T(8,128)(2,1)} %get-tuple-element.53.k_ref, ...), custom_call_target="tpu_custom_call" | custom-call | flops 40000000000 | bytes 20000000 | tf_op jit(solution)/shard_map/attention_backward/pallas_call | solution.py:200
  222.6 8.2 %weight_gradient.4 = (bf16[768,768]{1,0:T(8,128)(2,1)}, bf16[768,768]{1,0:T(8,128)(2,1)}, bf16[768,768]{1,0:T(8,128)(2,1)}) custom-call(bf16[1024,768]{1,0:T(8,128)(2,1)} %left_ref.1, bf16[1024,768]{1,0:T(8,128)(2,1)} %get-tuple-element.57.dq_ref.refs_0_, bf16[1024,768]{1,0:T(8,128)(2,1)} %get-tuple-element.58.dk_ref.refs_1_, ...), custom_call_target="tpu_custom_call" | custom-call | flops 5435817984 | bytes 9830400 | tf_op jit(solution)/shard_map/weight_gradient/pallas_call | solution.py:334
  230.8 4.9 pad_maximum_fusion
  235.7 0.0 reduce-scatter.12.cloned.1.call-update
  235.7 0.0 reduce-scatter.16.cloned.1.call-start
  235.8 9.7 %weight_gradient.6 = bf16[768,3072]{1,0:T(8,128)(2,1)} custom-call(bf16[1024,768]{1,0:T(8,128)(2,1)} %get-tuple-element.64.left_ref, bf16[1024,3072]{1,0:T(8,128)(2,1)} %get-tuple-element.65.refs_0_), custom_call_target="tpu_custom_call" | custom-call | flops 7247757312 | bytes 12582912 | tf_op jit(solution)/shard_map/weight_gradient/pallas_call | solution.py:334
  245.4 0.0 reduce-scatter.16.cloned.1.call-update
  245.5 0.0 reduce-scatter.22.cloned.1.call-start
  245.5 10.2 %weight_gradient.7 = bf16[768,3072]{1,0:T(8,128)(2,1)} custom-call(bf16[1024,768]{1,0:T(8,128)(2,1)} %get-tuple-element.66.left_ref, bf16[1024,3072]{1,0:T(8,128)(2,1)} %get-tuple-element.48.a_ref.refs_0_), custom_call_target="tpu_custom_call" | custom-call | flops 7247757312 | bytes 12582912 | tf_op jit(solution)/shard_map/weight_gradient/pallas_call | solution.py:334
  255.7 6.7 %copy.45 = bf16[768,3072]{0,1:T(8,128)(2,1)} copy(bf16[768,3072]{1,0:T(8,128)(2,1)} %weight_gradient.7) | data formatting | bytes 9437184
  262.4 0.0 reduce-scatter.22.cloned.1.call-update
  262.4 0.0 reduce-scatter.24.cloned.1.call-start
  262.5 0.7 slice.34
  263.2 0.7 slice.35
  264.0 0.9 slice_reduce_fusion
  265.0 1.0 copy.47
  265.9 0.0 reduce-scatter.24.cloned.1.call-update
  266.0 0.0 reduce-scatter.14.cloned.1.call-start
  266.0 23.8 %reduce-scatter.12.cloned.1.call-done = bf16[96,3072]{1,0:T(8,128)(2,1)} async-done(((bf16[768,3072]{1,0:T(8,128)(2,1)}), bf16[96,3072]{1,0:T(8,128)(2,1)}) %reduce-scatter.12.cloned.1.call-update) | async-done | bytes 589840 | tf_op jit(solution)/shard_map/reduce_scatter | solution.py:422
  289.8 0.0 reduce-scatter.14.cloned.1.call-update
  289.8 0.0 reduce-scatter.18.cloned.1.call-start
  289.9 57.5 %reduce-scatter.16.cloned.1.call-done = bf16[96,3072]{1,0:T(8,128)(2,1)} async-done(((bf16[768,3072]{1,0:T(8,128)(2,1)}), bf16[96,3072]{1,0:T(8,128)(2,1)}) %reduce-scatter.16.cloned.1.call-update) | async-done | bytes 589840 | tf_op jit(solution)/shard_map/reduce_scatter | solution.py:420
  347.4 0.0 reduce-scatter.20.cloned.1.call-start
  347.5 57.1 %reduce-scatter.22.cloned.1.call-done = bf16[384,768]{1,0:T(8,128)(2,1)} async-done(((bf16[3072,768]{1,0:T(8,128)(2,1)}), bf16[384,768]{1,0:T(8,128)(2,1)}) %reduce-scatter.22.cloned.1.call-update) | async-done | bytes 589840
  404.6 2.1 copy.46
  406.7 0.0 reduce-scatter.20.cloned.1.call-update
  406.8 0.6 dynamic-slice
  408.0 33.8 %reduce-scatter.24.cloned.1.call-done = f32[96,12]{1,0:T(8,128)} async-done(((f32[768,12]{1,0:T(8,128)}), f32[96,12]{1,0:T(8,128)}) %reduce-scatter.24.cloned.1.call-update) | async-done | bytes 4624
  441.8 0.9 copy.48
  442.7 11.9 %all-reduce = f32[96,12]{0,1:T(8,128)S(1)} all-reduce(f32[96,12]{0,1:T(8,128)S(1)} %copy.48), channel_id=9, replica_groups=mesh['dp'=8,'shard'=4] {'shard'}, use_global_device_ids=true, to_apply=%region_10.0.clone | all-reduce | flops 1152 | bytes 9216
  454.6 0.6 multiply_reduce_fusion
  455.2 11.0 %reduce-scatter.14.cloned.1.call-done = bf16[96,768]{1,0:T(8,128)(2,1)} async-done(((bf16[96,3072]{1,0:T(8,128)(2,1)}), bf16[96,768]{1,0:T(8,128)(2,1)}) %reduce-scatter.14.cloned.1.call-update) | async-done | bytes 147472 | tf_op jit(solution)/shard_map/reduce_scatter | solution.py:422
  466.2 1.6 fusion.4
  467.8 21.2 %reduce-scatter.18.cloned.1.call-done = bf16[96,768]{1,0:T(8,128)(2,1)} async-done(((bf16[96,3072]{1,0:T(8,128)(2,1)}), bf16[96,768]{1,0:T(8,128)(2,1)}) %reduce-scatter.18.cloned.1.call-update) | async-done | bytes 147472 | tf_op jit(solution)/shard_map/reduce_scatter | solution.py:420
  489.0 1.6 fusion.5
  491.9 20.3 %reduce-scatter.20.cloned.1.call-done = bf16[192,384]{1,0:T(8,128)(2,1)} async-done(((bf16[768,384]{1,0:T(8,128)(2,1)}), bf16[192,384]{1,0:T(8,128)(2,1)}) %reduce-scatter.20.cloned.1.call-update) | async-done | bytes 147472 | tf_op jit(solution)/shard_map/reduce_scatter | solution.py:419
  512.2 1.6 fusion.6
  515.2 8.6 %input_gradient.1 = bf16[1024,768]{1,0:T(8,128)(2,1)} custom-call(f32[6]{0:T(128)} %scale_ref.7, f32[1024,768]{1,0:T(8,128)} %get-tuple-element.51.dh_ref, bf16[1024,768]{1,0:T(8,128)(2,1)} %get-tuple-element.57.dq_ref.refs_0_, bf16[1024,768]{1,0:T(8,128)(2,1)} %get-tuple-element.58.dk_ref.refs_1_, bf16[1024,768]{1,0:T(8,128)(2,1)} %get-tuple-element.59.dv_ref.refs_2_, ...), custom_call_target="tpu_custom_call" | custom-call | flops 8999999488 | bytes 12976128 | tf_op jit(solution)/shard_map/input_gradient/pallas_call | solution.py:362
  523.8 38.5 %psum.7 = f32[]{:T(128)} all-reduce(f32[]{:T(128)S(6)} %add.98), channel_id=1, replica_groups=mesh['dp'=8,'shard'=4] {'dp','shard'}, use_global_device_ids=true, to_apply=%region_12.0 | all-reduce | flops 1 | bytes 8 | tf_op jit(solution)/shard_map/psum | solution.py:433
  563.1 0.6 multiply_add_fusion.3
  563.7 1.2 multiply_add_fusion
  565.0 2.7 multiply_add_fusion.1
  (50 shorter events, 0.2 us)
Async XLA Ops:
  7.2 54.2 %copy-start.15 = (f32[96,3]{0,1:T(4,128)S(1)}, f32[96,3]{0,1:T(4,128)}, u32[]{:S(2)}) copy-start(f32[96,3]{0,1:T(4,128)} %param.42) | copy-start | bytes 3460
  7.2 76.1 %all-gather.6.cloned.1.call-start = ((), (), s32[]{:S(2)}) async-start(), calls=%async_computation.7 | async-start | bytes 5308416 | tf_op jit(solution)/shard_map/all_gather | solution.py:397
  27.4 83.3 %all-gather.8.cloned.1.call-start = ((), (), s32[]{:S(2)}) async-start(), calls=%async_computation.8 | async-start | bytes 5308416 | tf_op jit(solution)/shard_map/all_gather | solution.py:399
  44.2 104.5 %all-gather.10.cloned.1.call-start = ((), (), s32[]{:S(2)}) async-start(), calls=%async_computation.9 | async-start | bytes 5308416 | tf_op jit(solution)/shard_map/all_gather | solution.py:400
  61.3 228.4 %reduce-scatter.12.cloned.1.call-start = ((), (), s32[]{:S(2)}) async-start(), calls=%async_computation.10 | async-start | bytes 5308416 | tf_op jit(solution)/shard_map/reduce_scatter | solution.py:422
  222.6 8.3 %copy-start = (bf16[768,768]{1,0:T(8,128)(2,1)S(1)}, bf16[768,768]{1,0:T(8,128)(2,1)}, u32[]{:S(2)}) copy-start(bf16[768,768]{1,0:T(8,128)(2,1)} %weight_gradient.5) | copy-start | bytes 3538948
  235.7 111.7 %reduce-scatter.16.cloned.1.call-start = ((), (), s32[]{:S(2)}) async-start(), calls=%async_computation.12 | async-start | bytes 5308416 | tf_op jit(solution)/shard_map/reduce_scatter | solution.py:420
  245.5 159.1 %reduce-scatter.22.cloned.1.call-start = ((), (), s32[]{:S(2)}) async-start(), calls=%async_computation.15 | async-start | bytes 5308416
  262.4 2.5 copy-start.14
  262.4 144.3 %copy-start.19 = (u32[32]{0:T(128)S(1)}, u32[32]{0:T(128)}, u32[]{:S(2)}) copy-start(u32[32]{0:T(128)} %constant.28) | copy-start | bytes 388
  262.4 179.4 %reduce-scatter.24.cloned.1.call-start = ((), (), s32[]{:S(2)}) async-start(), calls=%async_computation.16 | async-start | bytes 442368
  266.0 200.2 %reduce-scatter.14.cloned.1.call-start = ((), (), s32[]{:S(2)}) async-start(), calls=%async_computation.11 | async-start | bytes 737280 | tf_op jit(solution)/shard_map/reduce_scatter | solution.py:422
  289.8 199.2 %reduce-scatter.18.cloned.1.call-start = ((), (), s32[]{:S(2)}) async-start(), calls=%async_computation.13 | async-start | bytes 737280 | tf_op jit(solution)/shard_map/reduce_scatter | solution.py:420
  347.4 164.7 %reduce-scatter.20.cloned.1.call-start = ((), (), s32[]{:S(2)}) async-start(), calls=%async_computation.14 | async-start | bytes 737280 | tf_op jit(solution)/shard_map/reduce_scatter | solution.py:419
  515.1 48.0 %copy-start.16 = (f32[96,3]{0,1:T(4,128)S(1)}, f32[96,3]{0,1:T(4,128)}, u32[]{:S(2)}) copy-start(f32[96,3]{0,1:T(4,128)} %param.45) | copy-start | bytes 3460
  515.1 48.0 %copy-start.17 = (f32[96,3]{0,1:T(4,128)S(1)}, f32[96,3]{0,1:T(4,128)}, u32[]{:S(2)}) copy-start(f32[96,3]{0,1:T(4,128)} %param.44) | copy-start | bytes 3460
  515.1 48.0 %copy-start.18 = (f32[96,3]{0,1:T(4,128)S(1)}, f32[96,3]{0,1:T(4,128)}, u32[]{:S(2)}) copy-start(f32[96,3]{0,1:T(4,128)} %param.43) | copy-start | bytes 3460
  515.1 48.6 %copy-start.1 = (bf16[192,384]{1,0:T(8,128)(2,1)S(1)}, bf16[192,384]{1,0:T(8,128)(2,1)}, u32[]{:S(2)}) copy-start(bf16[192,384]{1,0:T(8,128)(2,1)} %reduce-scatter.20.cloned.1.call-done) | copy-start | bytes 442372
  515.1 48.6 %copy-start.4 = (f32[384,192]{0,1:T(8,128)S(1)}, f32[384,192]{0,1:T(8,128)}, u32[]{:S(2)}) copy-start(f32[384,192]{0,1:T(8,128)} %param.41) | copy-start | bytes 884740
  515.1 48.6 %copy-start.5 = (f32[384,192]{0,1:T(8,128)S(1)}, f32[384,192]{0,1:T(8,128)}, u32[]{:S(2)}) copy-start(f32[384,192]{0,1:T(8,128)} %param.38) | copy-start | bytes 884740
  515.1 48.6 %copy-start.6 = (f32[384,192]{0,1:T(8,128)S(1)}, f32[384,192]{0,1:T(8,128)}, u32[]{:S(2)}) copy-start(f32[384,192]{0,1:T(8,128)} %param.40) | copy-start | bytes 884740
  515.1 48.6 %copy-start.7 = (f32[384,192]{0,1:T(8,128)S(1)}, f32[384,192]{0,1:T(8,128)}, u32[]{:S(2)}) copy-start(f32[384,192]{0,1:T(8,128)} %param.39) | copy-start | bytes 884740
  515.2 49.8 %copy-start.2 = (bf16[96,768]{1,0:T(8,128)(2,1)S(1)}, bf16[96,768]{1,0:T(8,128)(2,1)}, u32[]{:S(2)}) copy-start(bf16[96,768]{1,0:T(8,128)(2,1)} %reduce-scatter.14.cloned.1.call-done) | copy-start | bytes 442372
  515.2 49.8 %copy-start.3 = (bf16[96,768]{1,0:T(8,128)(2,1)S(1)}, bf16[96,768]{1,0:T(8,128)(2,1)}, u32[]{:S(2)}) copy-start(bf16[96,768]{1,0:T(8,128)(2,1)} %reduce-scatter.18.cloned.1.call-done) | copy-start | bytes 442372
  515.2 49.8 %copy-start.8 = (f32[96,768]{1,0:T(8,128)S(1)}, f32[96,768]{1,0:T(8,128)}, u32[]{:S(2)}) copy-start(f32[96,768]{1,0:T(8,128)} %param.37) | copy-start | bytes 884740
  515.2 49.8 %copy-start.9 = (f32[96,768]{1,0:T(8,128)S(1)}, f32[96,768]{1,0:T(8,128)}, u32[]{:S(2)}) copy-start(f32[96,768]{1,0:T(8,128)} %param.34) | copy-start | bytes 884740
  515.2 49.8 %copy-start.10 = (f32[96,768]{1,0:T(8,128)S(1)}, f32[96,768]{1,0:T(8,128)}, u32[]{:S(2)}) copy-start(f32[96,768]{1,0:T(8,128)} %param.36) | copy-start | bytes 884740
  515.2 49.7 %copy-start.11 = (f32[96,768]{1,0:T(8,128)S(1)}, f32[96,768]{1,0:T(8,128)}, u32[]{:S(2)}) copy-start(f32[96,768]{1,0:T(8,128)} %param.35) | copy-start | bytes 884740
  515.2 49.7 %copy-start.12 = (f32[96,768]{1,0:T(8,128)S(1)}, f32[96,768]{1,0:T(8,128)}, u32[]{:S(2)}) copy-start(f32[96,768]{1,0:T(8,128)} %param.30) | copy-start | bytes 884740
  515.2 49.7 %copy-start.13 = (f32[96,768]{1,0:T(8,128)S(1)}, f32[96,768]{1,0:T(8,128)}, u32[]{:S(2)}) copy-start(f32[96,768]{1,0:T(8,128)} %param.32) | copy-start | bytes 884740
Sparse Core Ops, SparseCore 0:
  27.6 38.5 all-gather.5
  68.1 38.9 all-gather.7
  108.9 39.7 all-gather.9
  235.8 53.8 reduce-scatter.11
  293.5 53.8 reduce-scatter.15
  350.7 53.8 reduce-scatter.21
  408.0 33.8 reduce-scatter.23
  444.2 21.9 reduce-scatter.13
  468.6 20.3 reduce-scatter.17
  491.8 20.3 reduce-scatter.19
